TPU v7x, 256 devices: a whole 4x4x8 slice. The times are simulated.
256 devices in a mesh: row: 16 (over x, z_lo, core), col: 16 (over z_hi, y).
Axes of the slice: x: 4, y: 4, z: 8 (z_hi: 4, z_lo: 2; z = z_hi * 2 + z_lo), core: 2. Of those that a mesh axis runs over, the one named last changes fastest.
Arguments:
- frames_in: bfloat16 [4, 128, 128, 256], P(None, 'row', 'col'), may hold values from -6 to 6
- norm_gain: float32 [256], replicated, may hold values from 0.1 to 1.9
- first_kernel: bfloat16 [3, 3, 3, 256, 256], replicated, may hold values from -0.078125 to 0.078125
- second_kernel: bfloat16 [3, 3, 3, 256, 256], replicated, may hold values from -0.078125 to 0.078125
- latent_kernel: bfloat16 [3, 3, 4096, 1024], P(None, None, None, 'col'), may hold values from -0.03125 to 0.03125
Outputs:
- encoded: bfloat16 [4, 32, 32, 1024], P(None, 'row', None, 'col')
All inputs are finite; a program needn't handle non-finite values.
Results may differ from a plain program's by a relative error of at most 0.0053.
Values may be sent and summed in bfloat16 or wider, within the bound.
A program may use at most 128 MiB of HBM per device.

v0:
```python
import jax
import jax.numpy as jnp
from jax import lax
from jax.sharding import PartitionSpec as P

OUT_CH = 1024
LATENT = 4096


def with_halo(block, sides, width):
    for axis, dim in sides:
        count = lax.axis_size(axis)
        forward = [(i, i + 1) for i in range(count - 1)]
        backward = [(target, source) for source, target in forward]
        low = lax.ppermute(
            lax.slice_in_dim(block, block.shape[dim] - width, None, axis=dim), axis, forward
        )
        high = lax.ppermute(lax.slice_in_dim(block, 0, width, axis=dim), axis, backward)
        block = jnp.concatenate([low, block, high], axis=dim)
    return block


def conv_volume(padded, kernel, rows, cols):
    frames = padded.shape[0]
    chans = padded.shape[3]
    framed = jnp.pad(padded, ((1, 1), (0, 0), (0, 0), (0, 0)))
    total = jnp.zeros((frames * rows * cols, kernel.shape[4]), jnp.float32)
    for a in range(3):
        for b in range(3):
            for e in range(3):
                piece = framed[a : a + frames, b : b + rows, e : e + cols].reshape(-1, chans)
                total = total + jnp.dot(piece, kernel[a, b, e], preferred_element_type=jnp.float32)
    return total.reshape(frames, rows, cols, -1)


def per_device(frames_in, norm_gain, first_kernel, second_kernel, latent_kernel):
    frames, rows, cols, chans = frames_in.shape
    values = frames_in.astype(jnp.float32)
    scale = lax.rsqrt(jnp.mean(values * values, axis=-1, keepdims=True) + 1e-06)
    normed = (values * scale * norm_gain).astype(jnp.bfloat16)
    bordered = with_halo(normed, (("row", 1), ("col", 2)), 1)
    hidden = jax.nn.silu(conv_volume(bordered, first_kernel, rows, cols)).astype(jnp.bfloat16)
    hidden_border = with_halo(hidden, (("row", 1), ("col", 2)), 1)
    mixed = (values + conv_volume(hidden_border, second_kernel, rows, cols)).astype(jnp.bfloat16)
    latent = mixed.reshape(frames, rows // 4, 4, cols // 4, 4, chans)
    latent = latent.transpose(0, 1, 3, 2, 4, 5).reshape(frames, rows // 4, cols // 4, 16 * chans)
    gathered = lax.all_gather(latent, "col", axis=2, tiled=True)
    rimmed = with_halo(gathered, (("row", 1),), 1)
    lrows = rows // 4
    lcols = rimmed.shape[2]
    width_latent = rimmed.shape[3]
    padded = jnp.pad(rimmed, ((0, 0), (0, 0), (1, 1), (0, 0)))
    outs_dev = latent_kernel.shape[3]
    positions = frames * lrows * lcols
    total = jnp.zeros((outs_dev, positions), jnp.float32)
    for b in range(3):
        for e in range(3):
            piece = padded[:, b : b + lrows, e : e + lcols].reshape(-1, width_latent)
            total = total + lax.dot_general(
                latent_kernel[b, e],
                piece,
                (((0,), (1,)), ((), ())),
                preferred_element_type=jnp.float32,
            )
    group = LATENT // OUT_CH
    centre = rimmed[:, 1 : 1 + lrows]
    own_channels = lax.dynamic_slice_in_dim(
        centre, lax.axis_index("col") * outs_dev * group, outs_dev * group, 3
    )
    shortcut = jnp.mean(
        own_channels.astype(jnp.float32).reshape(frames, lrows, lcols, outs_dev, group), axis=-1
    )
    encoded = total.T.reshape(frames, lrows, lcols, outs_dev) + shortcut
    return encoded.astype(jnp.bfloat16)


def solution(mesh):
    return jax.shard_map(
        per_device,
        mesh=mesh,
        in_specs=(P(None, "row", "col", None), P(), P(), P(), P(None, None, None, "col")),
        out_specs=P(None, "row", None, "col"),
        check_vma=False,
    )
```

profile of v0, /device:TPU:1, one launch (start us, length us, event | category | flops | bytes accessed | tf_op | source)
XLA Modules:
  0.0 181.5 jit_solution(14845340982753075656)
XLA Ops:
  6.5 1.2 fusion.66
  7.7 1.0 fusion.68
  8.8 4.9 %collective-permute-start = (bf16[4,1,8,256]{3,2,1,0:T(8,128)(2,1)S(1)}, bf16[4,1,8,256]{3,2,1,0:T(8,128)(2,1)S(1)}, u32[]{:S(2)}, u32[]{:S(2)}) collective-permute-start(bf16[4,1,8,256]{3,2,1,0:T(8,128)(2,1)S(1)} %get-tuple-element.77), channel_id=1, source_target_pairs={{0,16},{16,32},{32,48},{48,64},{64,80},{80,96},{96,112},{112,128},... | collective-permute-start | bytes 49160 | tf_op jit(solution)/shard_map/ppermute | solution.py:15
  13.7 1.9 %collective-permute-start.1 = (bf16[4,1,8,256]{3,2,1,0:T(8,128)(2,1)S(1)}, bf16[4,1,8,256]{3,2,1,0:T(8,128)(2,1)S(1)}, u32[]{:S(2)}, u32[]{:S(2)}) collective-permute-start(bf16[4,1,8,256]{3,2,1,0:T(8,128)(2,1)S(1)} %get-tuple-element.78), channel_id=1, source_target_pairs={{16,0},{32,16},{48,32},{64,48},{80,64},{96,80},{112,96},{128,112},... | collective-permute-start | bytes 49160 | tf_op jit(solution)/shard_map/ppermute | solution.py:18
  15.6 3.1 %collective-permute-done.1 = bf16[4,1,8,256]{3,2,1,0:T(8,128)(2,1)S(1)} collective-permute-done((bf16[4,1,8,256]{3,2,1,0:T(8,128)(2,1)S(1)}, bf16[4,1,8,256]{3,2,1,0:T(8,128)(2,1)S(1)}, u32[]{:S(2)}, u32[]{:S(2)}) %collective-permute-start.1) | collective-permute-done | bytes 16416 | tf_op jit(solution)/shard_map/ppermute | solution.py:18
  18.8 3.2 %collective-permute-start.2 = (bf16[4,10,1,256]{3,2,1,0:T(2,128)(2,1)S(1)}, bf16[4,10,1,256]{3,2,1,0:T(2,128)(2,1)S(1)}, u32[]{:S(2)}, u32[]{:S(2)}) collective-permute-start(bf16[4,10,1,256]{3,2,1,0:T(2,128)(2,1)S(1)} %get-tuple-element.69), channel_id=1, source_target_pairs={{0,1},{1,2},{2,3},{3,4},{4,5},{5,6},{6,7},{7,8},{8,9},{9,10},{10,1... | collective-permute-start | bytes 61448 | tf_op jit(solution)/shard_map/ppermute | solution.py:15
  22.0 1.3 collective-permute-start.3
  23.4 3.4 %collective-permute-done.3 = bf16[4,10,1,256]{3,2,1,0:T(2,128)(2,1)S(1)} collective-permute-done((bf16[4,10,1,256]{3,2,1,0:T(2,128)(2,1)S(1)}, bf16[4,10,1,256]{3,2,1,0:T(2,128)(2,1)S(1)}, u32[]{:S(2)}, u32[]{:S(2)}) %collective-permute-start.3) | collective-permute-done | bytes 20512 | tf_op jit(solution)/shard_map/ppermute | solution.py:18
  26.8 0.2 maximum_maximum_fusion
  27.4 0.2 fusion.61
  27.6 0.3 fusion.189
  28.2 0.2 convolution_add_fusion.47
  29.9 0.2 fusion.9
  30.1 0.2 convolution_add_fusion.37
  30.3 0.2 convolution_add_fusion.36
  30.7 0.2 convolution_add_fusion.34
  30.9 0.2 fusion.8
  31.3 0.2 convolution_add_fusion.31
  31.5 0.2 convolution_add_fusion.30
  31.7 0.2 convolution_add_fusion.29
  31.9 0.2 convolution_add_fusion.28
  32.1 0.2 convolution_add_fusion.27
  33.0 3.5 %collective-permute-start.4 = (bf16[4,1,8,256]{3,2,1,0:T(8,128)(2,1)S(1)}, bf16[4,1,8,256]{3,2,1,0:T(8,128)(2,1)S(1)}, u32[]{:S(2)}, u32[]{:S(2)}) collective-permute-start(bf16[4,1,8,256]{3,2,1,0:T(8,128)(2,1)S(1)} %get-tuple-element.73), channel_id=1, source_target_pairs={{0,16},{16,32},{32,48},{48,64},{64,80},{80,96},{96,112},{112,128},... | collective-permute-start | bytes 49160 | tf_op jit(solution)/shard_map/ppermute | solution.py:15
  36.5 1.9 %collective-permute-start.5 = (bf16[4,1,8,256]{3,2,1,0:T(8,128)(2,1)S(1)}, bf16[4,1,8,256]{3,2,1,0:T(8,128)(2,1)S(1)}, u32[]{:S(2)}, u32[]{:S(2)}) collective-permute-start(bf16[4,1,8,256]{3,2,1,0:T(8,128)(2,1)S(1)} %get-tuple-element.74), channel_id=1, source_target_pairs={{16,0},{32,16},{48,32},{64,48},{80,64},{96,80},{112,96},{128,112},... | collective-permute-start | bytes 49160 | tf_op jit(solution)/shard_map/ppermute | solution.py:18
  38.4 3.1 %collective-permute-done.5 = bf16[4,1,8,256]{3,2,1,0:T(8,128)(2,1)S(1)} collective-permute-done((bf16[4,1,8,256]{3,2,1,0:T(8,128)(2,1)S(1)}, bf16[4,1,8,256]{3,2,1,0:T(8,128)(2,1)S(1)}, u32[]{:S(2)}, u32[]{:S(2)}) %collective-permute-start.5) | collective-permute-done | bytes 16416 | tf_op jit(solution)/shard_map/ppermute | solution.py:18
  41.6 3.2 %collective-permute-start.6 = (bf16[4,10,1,256]{3,2,1,0:T(2,128)(2,1)S(1)}, bf16[4,10,1,256]{3,2,1,0:T(2,128)(2,1)S(1)}, u32[]{:S(2)}, u32[]{:S(2)}) collective-permute-start(bf16[4,10,1,256]{3,2,1,0:T(2,128)(2,1)S(1)} %get-tuple-element.65), channel_id=1, source_target_pairs={{0,1},{1,2},{2,3},{3,4},{4,5},{5,6},{6,7},{7,8},{8,9},{9,10},{10,1... | collective-permute-start | bytes 61448 | tf_op jit(solution)/shard_map/ppermute | solution.py:15
  44.8 1.3 collective-permute-start.7
  46.1 3.9 %collective-permute-done.7 = bf16[4,10,1,256]{3,2,1,0:T(2,128)(2,1)S(1)} collective-permute-done((bf16[4,10,1,256]{3,2,1,0:T(2,128)(2,1)S(1)}, bf16[4,10,1,256]{3,2,1,0:T(2,128)(2,1)S(1)}, u32[]{:S(2)}, u32[]{:S(2)}) %collective-permute-start.7) | collective-permute-done | bytes 20512 | tf_op jit(solution)/shard_map/ppermute | solution.py:18
  50.0 0.2 maximum_maximum_fusion.1
  50.7 0.2 select_maximum_fusion
  50.9 0.3 fusion.188
  51.4 0.2 convolution_add_fusion.23
  51.6 0.2 convolution_add_fusion.22
  51.8 0.2 convolution_add_fusion.21
  52.2 0.2 convolution_add_fusion.19
  52.6 0.2 convolution_add_fusion.17
  53.2 0.2 fusion.7
  53.6 0.2 convolution_add_fusion.12
  54.2 0.2 fusion.6
  54.4 0.2 convolution_add_fusion.8
  54.8 0.2 convolution_add_fusion.6
  56.3 0.7 copy.29
  57.1 69.1 %all-gather.2.cloned.1.call-done = bf16[4,2,32,4096]{3,0,1,2:T(4,128)(2,1)} async-done(((bf16[4,2,2,4096]{3,0,1,2:T(4,128)(2,1)}), bf16[4,2,32,4096]{3,0,1,2:T(4,128)(2,1)}) %all-gather.2.cloned.1.call-update) | async-done | bytes 2097168 | tf_op jit(solution)/shard_map/all_gather | solution.py:47
  126.2 2.7 %copy.30 = bf16[4,2,32,4096]{3,2,1,0:T(8,128)(2,1)S(1)} copy(bf16[4,2,32,4096]{3,0,1,2:T(4,128)(2,1)} %all-gather.2.cloned.1.call-done) | data formatting | bytes 4194304 | tf_op jit(solution)/shard_map/all_gather | solution.py:47
  129.0 1.5 fusion.187
  130.4 2.7 %collective-permute-start.8 = (bf16[4,1,32,4096]{3,2,1,0:T(8,128)(2,1)}, bf16[4,1,32,4096]{3,2,1,0:T(8,128)(2,1)}, u32[]{:S(2)}, u32[]{:S(2)}) collective-permute-start(bf16[4,1,32,4096]{3,2,1,0:T(8,128)(2,1)} %get-tuple-element.13), channel_id=1, source_target_pairs={{0,16},{16,32},{32,48},{48,64},{64,80},{80,96},{96,112},{112,128},... | collective-permute-start | bytes 3145736 | tf_op jit(solution)/shard_map/ppermute | solution.py:15
  133.2 2.7 %collective-permute-start.9 = (bf16[4,1,32,4096]{3,2,1,0:T(8,128)(2,1)}, bf16[4,1,32,4096]{3,2,1,0:T(8,128)(2,1)}, u32[]{:S(2)}, u32[]{:S(2)}) collective-permute-start(bf16[4,1,32,4096]{3,2,1,0:T(8,128)(2,1)} %get-tuple-element.14), channel_id=1, source_target_pairs={{16,0},{32,16},{48,32},{64,48},{80,64},{96,80},{112,96},{128,112},... | collective-permute-start | bytes 3145736 | tf_op jit(solution)/shard_map/ppermute | solution.py:18
  135.9 0.3 copy.38
  136.3 0.6 reduce_sum.19
  137.1 2.0 %fusion.21 = f32[256,64]{0,1:T(8,128)S(1)} fusion(bf16[256,4096]{1,0:T(8,128)(2,1)S(1)} %bitcast.330, bf16[3,3,4096,64]{2,3,1,0:T(8,128)(2,1)} %param.9), kind=kOutput, calls=%fused_computation.76 | convolution fusion | flops 134217728 | bytes 2686976 | tf_op jit(solution)/shard_map/dot_general | solution.py:59
  139.0 6.2 %collective-permute-done.8 = bf16[4,1,32,4096]{3,2,1,0:T(8,128)(2,1)} collective-permute-done((bf16[4,1,32,4096]{3,2,1,0:T(8,128)(2,1)}, bf16[4,1,32,4096]{3,2,1,0:T(8,128)(2,1)}, u32[]{:S(2)}, u32[]{:S(2)}) %collective-permute-start.8) | collective-permute-done | bytes 1048608 | tf_op jit(solution)/shard_map/ppermute | solution.py:15
  145.2 13.8 %collective-permute-done.9 = bf16[4,1,32,4096]{3,2,1,0:T(8,128)(2,1)} collective-permute-done((bf16[4,1,32,4096]{3,2,1,0:T(8,128)(2,1)}, bf16[4,1,32,4096]{3,2,1,0:T(8,128)(2,1)}, u32[]{:S(2)}, u32[]{:S(2)}) %collective-permute-start.9) | collective-permute-done | bytes 1048608 | tf_op jit(solution)/shard_map/ppermute | solution.py:18
  159.0 1.9 %pad_maximum_fusion.1 = (bf16[4,2,32,4096]{3,2,1,0:T(8,128)(2,1)S(1)}, bf16[4,2,32,4096]{3,2,1,0:T(8,128)(2,1)S(1)}) fusion(bf16[4,2,32,4096]{3,2,1,0:T(8,128)(2,1)S(1)} %copy.30, bf16[4,1,32,4096]{3,2,1,0:T(8,128)(2,1)} %collective-permute-done.8, bf16[4,1,32,4096]{3,2,1,0:T(8,128)(2,1)} %collective-permute-done.9), kind=kLoop, calls=%fused_computation.9 | loop fusion | flops 2097152 | bytes 8388608 | tf_op jit(solution)/shard_map/concatenate | solution.py:19
  161.0 0.8 fusion.27
  161.7 0.8 fusion.16
  162.5 3.7 %fusion.5 = bf16[4,4,34,4096]{3,2,1,0:T(8,128)(2,1)S(1)} fusion(bf16[4,1,32,4096]{3,2,1,0:T(8,128)(2,1)} %collective-permute-done.9, bf16[4,2,32,4096]{3,2,1,0:T(8,128)(2,1)S(1)} %copy.30, bf16[4,1,32,4096]{3,2,1,0:T(8,128)(2,1)} %collective-permute-done.8), kind=kLoop, calls=%fused_computation.7 | loop fusion | flops 26738688 | bytes 8650752 | tf_op jit(solution)/shard_map/concatenate | solution.py:19
  166.2 3.1 %fusion.186 = (bf16[4,2,32,4096]{3,2,1,0:T(8,128)(2,1)S(1)}, bf16[4,2,32,4096]{3,2,1,0:T(8,128)(2,1)S(1)}, bf16[4,2,32,4096]{3,2,1,0:T(8,128)(2,1)S(1)}, bf16[4,...) fusion(bf16[4,4,34,4096]{3,2,1,0:T(8,128)(2,1)S(1)} %fusion.5), kind=kLoop, calls=%fused_computation.258 | loop fusion | bytes 25165824 | tf_op jit(solution)/shard_map/slice | solution.py:58
  169.3 0.8 fusion.18
  170.1 0.8 fusion.23
  170.8 0.8 fusion.25
  171.6 0.8 fusion.14
  172.4 0.8 fusion.40
  173.1 0.8 fusion.12
  174.0 0.7 add_convert_fusion
  (68 shorter events, 7.0 us)
Async XLA Ops:
  6.5 20.5 %copy-start = (bf16[3,3,3,256,256]{4,3,2,1,0:T(8,128)(2,1)S(1)}, bf16[3,3,3,256,256]{4,3,2,1,0:T(8,128)(2,1)}, u32[]{:S(2)}) copy-start(bf16[3,3,3,256,256]{4,3,2,1,0:T(8,128)(2,1)} %param.7) | copy-start | bytes 10616836
  6.5 119.7 %all-gather.2.cloned.1.call-start = ((), (), s32[]{:S(2)}) async-start(), calls=%async_computation | async-start | bytes 2228224 | tf_op jit(solution)/shard_map/all_gather | solution.py:47
  8.8 6.9 %collective-permute-start = (bf16[4,1,8,256]{3,2,1,0:T(8,128)(2,1)S(1)}, bf16[4,1,8,256]{3,2,1,0:T(8,128)(2,1)S(1)}, u32[]{:S(2)}, u32[]{:S(2)}) collective-permute-start(bf16[4,1,8,256]{3,2,1,0:T(8,128)(2,1)S(1)} %get-tuple-element.77), channel_id=1, source_target_pairs={{0,16},{16,32},{32,48},{48,64},{64,80},{80,96},{96,112},{112,128},... | collective-permute-start | bytes 49160 | tf_op jit(solution)/shard_map/ppermute | solution.py:15
  13.7 5.1 %collective-permute-start.1 = (bf16[4,1,8,256]{3,2,1,0:T(8,128)(2,1)S(1)}, bf16[4,1,8,256]{3,2,1,0:T(8,128)(2,1)S(1)}, u32[]{:S(2)}, u32[]{:S(2)}) collective-permute-start(bf16[4,1,8,256]{3,2,1,0:T(8,128)(2,1)S(1)} %get-tuple-element.78), channel_id=1, source_target_pairs={{16,0},{32,16},{48,32},{64,48},{80,64},{96,80},{112,96},{128,112},... | collective-permute-start | bytes 49160 | tf_op jit(solution)/shard_map/ppermute | solution.py:18
  18.8 4.5 %collective-permute-start.2 = (bf16[4,10,1,256]{3,2,1,0:T(2,128)(2,1)S(1)}, bf16[4,10,1,256]{3,2,1,0:T(2,128)(2,1)S(1)}, u32[]{:S(2)}, u32[]{:S(2)}) collective-permute-start(bf16[4,10,1,256]{3,2,1,0:T(2,128)(2,1)S(1)} %get-tuple-element.69), channel_id=1, source_target_pairs={{0,1},{1,2},{2,3},{3,4},{4,5},{5,6},{6,7},{7,8},{8,9},{9,10},{10,1... | collective-permute-start | bytes 61448 | tf_op jit(solution)/shard_map/ppermute | solution.py:15
  22.0 4.7 %collective-permute-start.3 = (bf16[4,10,1,256]{3,2,1,0:T(2,128)(2,1)S(1)}, bf16[4,10,1,256]{3,2,1,0:T(2,128)(2,1)S(1)}, u32[]{:S(2)}, u32[]{:S(2)}) collective-permute-start(bf16[4,10,1,256]{3,2,1,0:T(2,128)(2,1)S(1)} %get-tuple-element.70), channel_id=1, source_target_pairs={{1,0},{2,1},{3,2},{4,3},{5,4},{6,5},{7,6},{8,7},{9,8},{10,9},{11,1... | collective-permute-start | bytes 61448 | tf_op jit(solution)/shard_map/ppermute | solution.py:18
  32.1 18.2 %copy-start.1 = (bf16[3,3,3,256,256]{4,3,2,1,0:T(8,128)(2,1)S(1)}, bf16[3,3,3,256,256]{4,3,2,1,0:T(8,128)(2,1)}, u32[]{:S(2)}) copy-start(bf16[3,3,3,256,256]{4,3,2,1,0:T(8,128)(2,1)} %param.8) | copy-start | bytes 10616836
  33.0 5.4 %collective-permute-start.4 = (bf16[4,1,8,256]{3,2,1,0:T(8,128)(2,1)S(1)}, bf16[4,1,8,256]{3,2,1,0:T(8,128)(2,1)S(1)}, u32[]{:S(2)}, u32[]{:S(2)}) collective-permute-start(bf16[4,1,8,256]{3,2,1,0:T(8,128)(2,1)S(1)} %get-tuple-element.73), channel_id=1, source_target_pairs={{0,16},{16,32},{32,48},{48,64},{64,80},{80,96},{96,112},{112,128},... | collective-permute-start | bytes 49160 | tf_op jit(solution)/shard_map/ppermute | solution.py:15
  36.5 5.1 %collective-permute-start.5 = (bf16[4,1,8,256]{3,2,1,0:T(8,128)(2,1)S(1)}, bf16[4,1,8,256]{3,2,1,0:T(8,128)(2,1)S(1)}, u32[]{:S(2)}, u32[]{:S(2)}) collective-permute-start(bf16[4,1,8,256]{3,2,1,0:T(8,128)(2,1)S(1)} %get-tuple-element.74), channel_id=1, source_target_pairs={{16,0},{32,16},{48,32},{64,48},{80,64},{96,80},{112,96},{128,112},... | collective-permute-start | bytes 49160 | tf_op jit(solution)/shard_map/ppermute | solution.py:18
  41.6 4.5 %collective-permute-start.6 = (bf16[4,10,1,256]{3,2,1,0:T(2,128)(2,1)S(1)}, bf16[4,10,1,256]{3,2,1,0:T(2,128)(2,1)S(1)}, u32[]{:S(2)}, u32[]{:S(2)}) collective-permute-start(bf16[4,10,1,256]{3,2,1,0:T(2,128)(2,1)S(1)} %get-tuple-element.65), channel_id=1, source_target_pairs={{0,1},{1,2},{2,3},{3,4},{4,5},{5,6},{6,7},{7,8},{8,9},{9,10},{10,1... | collective-permute-start | bytes 61448 | tf_op jit(solution)/shard_map/ppermute | solution.py:15
  44.8 5.2 %collective-permute-start.7 = (bf16[4,10,1,256]{3,2,1,0:T(2,128)(2,1)S(1)}, bf16[4,10,1,256]{3,2,1,0:T(2,128)(2,1)S(1)}, u32[]{:S(2)}, u32[]{:S(2)}) collective-permute-start(bf16[4,10,1,256]{3,2,1,0:T(2,128)(2,1)S(1)} %get-tuple-element.66), channel_id=1, source_target_pairs={{1,0},{2,1},{3,2},{4,3},{5,4},{6,5},{7,6},{8,7},{9,8},{10,9},{11,1... | collective-permute-start | bytes 61448 | tf_op jit(solution)/shard_map/ppermute | solution.py:18
  54.4 1.8 copy-start.2
  130.4 14.8 %collective-permute-start.8 = (bf16[4,1,32,4096]{3,2,1,0:T(8,128)(2,1)}, bf16[4,1,32,4096]{3,2,1,0:T(8,128)(2,1)}, u32[]{:S(2)}, u32[]{:S(2)}) collective-permute-start(bf16[4,1,32,4096]{3,2,1,0:T(8,128)(2,1)} %get-tuple-element.13), channel_id=1, source_target_pairs={{0,16},{16,32},{32,48},{48,64},{64,80},{80,96},{96,112},{112,128},... | collective-permute-start | bytes 3145736 | tf_op jit(solution)/shard_map/ppermute | solution.py:15
  133.2 25.8 %collective-permute-start.9 = (bf16[4,1,32,4096]{3,2,1,0:T(8,128)(2,1)}, bf16[4,1,32,4096]{3,2,1,0:T(8,128)(2,1)}, u32[]{:S(2)}, u32[]{:S(2)}) collective-permute-start(bf16[4,1,32,4096]{3,2,1,0:T(8,128)(2,1)} %get-tuple-element.14), channel_id=1, source_target_pairs={{16,0},{32,16},{48,32},{64,48},{80,64},{96,80},{112,96},{128,112},... | collective-permute-start | bytes 3145736 | tf_op jit(solution)/shard_map/ppermute | solution.py:18
  137.1 23.9 %slice-start = ((s8[4718592]{0:T(1024)(128)(4,1)}), s8[4194304]{0:T(1024)(128)(4,1)S(1)}, s32[]{:S(2)}) async-start(s8[4718592]{0:T(1024)(128)(4,1)} %bitcast.340), calls=%async_computation.1 | async-start | bytes 8388608
  139.0 21.9 %slice-start.1 = ((s8[4718592]{0:T(1024)(128)(4,1)}), s8[524288]{0:T(1024)(128)(4,1)S(1)}, s32[]{:S(2)}) async-start(s8[4718592]{0:T(1024)(128)(4,1)} %bitcast.340), calls=%async_computation.2 | async-start | bytes 1048576
Sparse Core Ops, SparseCore 0:
  57.2 68.9 all-gather.1
where the time goes:
time: 182 us
  waiting for transfers between devices  103 us (57%)
  starting transfers between devices  26.7 us (15%)
  matrix products  18.2 us (10%)
  between operations  14.2 us (8%)
  other arithmetic  10.1 us (6%)
  local copies, waits for them, and re-layouts  9.65 us (5%)
    all_gather x1, waiting for transfers between devices, per_device(): gathered = lax.all_gather(latent, 'col', axis=2, tiled=True)  69.1 us
    ppermute x5, waiting for transfers between devices, with_halo(): lax.ppermute(lax.slice_in_dim(block, 0, width, axis=dim), axis, backward)  27.3 us
    ppermute x5, starting transfers between devices, with_halo(): lax.ppermute(lax.slice_in_dim(block, block.shape[dim] - width, None, axis...  17.6 us
    dot_general x54, matrix products, conv_volume(): jnp.dot(piece, kernel[a, b, e], preferred_element_type=jnp.float32)  10.1 us
    ppermute x5, starting transfers between devices, with_halo(): lax.ppermute(lax.slice_in_dim(block, 0, width, axis=dim), axis, backward)  9.14 us
    dot_general x9, matrix products, per_device(): lax.dot_general(latent_kernel[b, e], piece, (((0,), (1,)), ((), ())), pre...  8.07 us
    concatenate x8, other arithmetic, with_halo(): block = jnp.concatenate([low, block, high], axis=dim)  6.4 us
    ppermute x5, waiting for transfers between devices, with_halo(): lax.ppermute(lax.slice_in_dim(block, block.shape[dim] - width, None, axis...  6.2 us
  transfers between devices with their start and end apart: 11, of which 7 were waited for; matrix products, arithmetic and copies ran while one was open for 2% of the time, Pallas kernels for 0%

commit v1 on v0

v1 whole, which is shorter than its diff:
```python
import functools

import jax
import jax.numpy as jnp
import numpy as np
from jax import lax
from jax.experimental import pallas as pl
from jax.experimental.pallas import tpu as pltpu
from jax.sharding import PartitionSpec as P

MESH = pl.DeviceIdType.MESH
F32 = jnp.float32
BF16 = jnp.bfloat16
FRAMES, SIDE, CHANS = 4, 8, 256
OUT_CH, LATENT = 1024, 4096
RING = 4
PIECES = RING * RING
CHUNKS = 8
CHUNK = LATENT // CHUNKS
OUT_DEV = OUT_CH // PIECES
Y_FIRST = (False,) * CHUNKS


def one_hot(index, width):
    out = np.zeros((len(index), width), np.float32)
    for at, source in enumerate(index):
        if source >= 0:
            out[at, source] = 1
    return out.astype(BF16)


def spread_tables():
    own, halo = [], []
    for p in range(-2, 6):
        for q in range(-2, 6):
            for i in range(2):
                for f in range(FRAMES):
                    for j in range(2):
                        r, c = 4 * i + p, 4 * j + q
                        inside_r, inside_c = 0 <= r < SIDE, 0 <= c < SIDE
                        a, b = -1, -1
                        side = 0 if c < 0 else 1
                        cc = c + 2 if c < 0 else c - SIDE
                        rr = r + 2 if r < 0 else r - SIDE
                        if inside_r and inside_c:
                            a = f * 64 + r * 8 + c
                        elif inside_c:
                            b = ((0 if r < 0 else 4) + f) * 16 + rr * 8 + c
                        elif inside_r:
                            b = (8 + 4 * side + r // 2) * 16 + f * 4 + (r % 2) * 2 + cc
                        else:
                            b = (16 + (0 if r < 0 else 2) + side) * 16 + f * 4 + rr * 2 + cc
                        own.append(a)
                        halo.append(b)
    return one_hot(own, 256), one_hot(halo, 384)


def strip_table():
    index = []
    for side in range(2):
        for rp in range(4):
            for f in range(FRAMES):
                for rr in range(2):
                    for cc in range(2):
                        index.append(f * 64 + (2 * rp + rr) * 8 + 6 * side + cc)
    return one_hot(index, 256)


def mean_table():
    group = LATENT // OUT_CH
    out = np.zeros((CHANS, CHANS // group), np.float32)
    out[np.arange(CHANS), np.arange(CHANS) // group] = 1 / group
    return out.astype(BF16)


def convolve(src, w, n, acc):
    rows = n * n * 16
    for a in range(3):
        total = None
        for b in range(3):
            for e in range(3):
                part = jnp.dot(src[b : b + n, e : e + n].reshape(rows, CHANS), w[a, b, e], preferred_element_type=F32)
                total = part if total is None else total + part
        acc[a, :rows] = total


def joined(acc, rows):
    early, same, late = (acc[a, :rows].reshape(rows // 8, 8, CHANS) for a in range(3))
    f = lax.broadcasted_iota(jnp.int32, (1, 8, CHANS), 1) // 2
    return same + jnp.where(f > 0, pltpu.roll(early, 2, 1), 0.0) + jnp.where(f < FRAMES - 1, pltpu.roll(late, 6, 1), 0.0)


def kernel(
    n_row, n_col,
    x_hbm, gain_hbm, k1_hbm, k2_hbm, w_hbm, g_own_hbm, g_halo_hbm, g_strip_hbm, g_mean_hbm,
    out_ref,
    x, gain, k1, k2, w, g_own, g_halo, g_strip, g_mean,
    strips, halo, normed, cells, hidden, acc, lat, y_acc, u_out, u_in, kept,
    load_sem, w_sem, halo_send, halo_recv,
    near_send, near_recv, far_send, far_recv, near2_send, near2_recv, far2_send, far2_recv,
    u_send, u_recv,
):
    row, col = lax.axis_index("row"), lax.axis_index("col")
    zh, y = col // RING, col % RING
    up, down = lax.rem(row + n_row - 1, n_row), lax.rem(row + 1, n_row)
    left, right = lax.rem(col + n_col - 1, n_col), lax.rem(col + 1, n_col)
    z_next, z_prev = lax.rem(zh + 1, RING), lax.rem(zh + RING - 1, RING)
    y_next, y_prev = lax.rem(y + 1, RING), lax.rem(y + RING - 1, RING)
    to_z = ((row, z_next * RING + y), (row, z_prev * RING + y))
    to_y = ((row, zh * RING + y_next), (row, zh * RING + y_prev))

    barrier = pltpu.get_barrier_semaphore()
    around = (
        (up, col), (down, col), (row, left), (row, right),
        (up, left), (up, right), (down, left), (down, right),
    ) + to_z + to_y
    for target in around:
        pl.semaphore_signal(barrier, inc=1, device_id=target, device_id_type=MESH)

    loads = []
    for at, (source, target) in enumerate((
        (x_hbm, x), (g_strip_hbm, g_strip), (gain_hbm, gain), (g_own_hbm, g_own), (g_halo_hbm, g_halo),
        (k1_hbm, k1), (k2_hbm, k2), (g_mean_hbm, g_mean),
    )):
        copy = pltpu.make_async_copy(source, target, load_sem.at[at])
        copy.start()
        loads.append(copy)
    w_loads = []
    for b in range(3):
        for e in range(3):
            copy = pltpu.make_async_copy(w_hbm.at[b, e], w.at[e, pl.ds(b * OUT_DEV, OUT_DEV)], w_sem.at[b * 3 + e])
            copy.start()
            w_loads.append(copy)
    load_x, load_strip, load_gain, load_own, load_halo, load_k1, load_k2, load_mean = loads

    def send(source, target, send_sem, recv_sem, device):
        copy = pltpu.make_async_remote_copy(
            src_ref=source, dst_ref=target, send_sem=send_sem, recv_sem=recv_sem, device_id=device, device_id_type=MESH
        )
        copy.start()
        return copy

    load_x.wait()
    pl.semaphore_wait(barrier, len(around))
    sent = [
        send(x.at[:, 0], halo.at[pl.ds(4, 4)], halo_send.at[0], halo_recv.at[0], (up, col)),
        send(x.at[:, 3], halo.at[pl.ds(0, 4)], halo_send.at[1], halo_recv.at[1], (down, col)),
    ]
    load_strip.wait()
    own = x[...].reshape(256, CHANS)
    strips[...] = jnp.dot(g_strip[...], own, preferred_element_type=F32).astype(BF16).reshape(2, 4, 16, CHANS)
    sent += [
        send(strips.at[0, 3], halo.at[17], halo_send.at[4], halo_recv.at[4], (down, left)),
        send(strips.at[1, 3], halo.at[16], halo_send.at[5], halo_recv.at[5], (down, right)),
        send(strips.at[0, 0], halo.at[19], halo_send.at[6], halo_recv.at[6], (up, left)),
        send(strips.at[1, 0], halo.at[18], halo_send.at[7], halo_recv.at[7], (up, right)),
        send(strips.at[0], halo.at[pl.ds(12, 4)], halo_send.at[2], halo_recv.at[2], (row, left)),
        send(strips.at[1], halo.at[pl.ds(8, 4)], halo_send.at[3], halo_recv.at[3], (row, right)),
    ]

    load_gain.wait()

    def norm(raw):
        values = raw.astype(F32)
        scale = lax.rsqrt(jnp.mean(values * values, axis=-1, keepdims=True) + 1e-06)
        return values * scale * gain[...]

    normed[0:16] = norm(own).astype(BF16).reshape(16, 16, CHANS)
    normed[36:40] = jnp.zeros((4, 16, CHANS), BF16)
    load_own.wait()
    middle = g_own[...].reshape(8, 8, 16, 256)[2:6, 2:6].reshape(256, 256)
    kept[...] = jnp.dot(middle, own, preferred_element_type=F32)

    for copy in sent:
        copy.wait_recv()
    has_up, has_down = row > 0, row < n_row - 1
    has_left, has_right = col > 0, col < n_col - 1
    for start, count, there in (
        (0, 4, has_up), (4, 4, has_down), (8, 4, has_left), (12, 4, has_right),
        (16, 1, has_up & has_left), (17, 1, has_up & has_right),
        (18, 1, has_down & has_left), (19, 1, has_down & has_right),
    ):
        values = norm(halo[start : start + count].reshape(count * 16, CHANS))
        values = values * jnp.where(there, 1.0, 0.0).astype(F32)
        normed[16 + start : 16 + start + count] = values.astype(BF16).reshape(count, 16, CHANS)
    load_halo.wait()
    spread = jnp.dot(g_own[...], normed[0:16].reshape(256, CHANS), preferred_element_type=F32)
    spread += jnp.dot(g_halo[...], normed[16:40].reshape(384, CHANS), preferred_element_type=F32)
    cells[...] = spread.astype(BF16).reshape(8, 8, 16, CHANS)

    load_k1.wait()
    convolve(cells, k1, 6, acc)
    value = joined(acc, 576)
    value = (value / (1.0 + jnp.exp(-value))).reshape(6, 6, 2, 8, CHANS)
    hidden[...] = value.astype(BF16).reshape(6, 6, 16, CHANS)
    place = lax.broadcasted_iota(jnp.int32, (1, 16, CHANS), 1)
    i_of, j_of = place // 8, place % 2
    none = jnp.zeros((), BF16)
    for edge, outside, there in ((0, i_of == 0, has_up), (5, i_of == 1, has_down)):
        keep = jnp.logical_or(jnp.logical_not(outside), there)
        hidden[edge] = jnp.where(keep, hidden[edge].astype(F32), 0.0).astype(BF16)
    for edge, outside, there in ((0, j_of == 0, has_left), (5, j_of == 1, has_right)):
        keep = jnp.logical_or(jnp.logical_not(outside), there)
        hidden[:, edge] = jnp.where(keep, hidden[:, edge].astype(F32), 0.0).astype(BF16)

    load_k2.wait()
    convolve(hidden, k2, 4, acc)
    mixed = (kept[...].reshape(32, 8, CHANS) + joined(acc, 256)).astype(BF16).reshape(16, 16, CHANS)
    for tile in range(16):
        lat[tile // 2, zh, y, :, (tile % 2) * CHANS : (tile % 2 + 1) * CHANS] = mixed[tile]

    opposite_z, opposite_y = lax.rem(zh + 2, RING), lax.rem(y + 2, RING)
    pending = []
    near, far, near2, far2 = [None] * CHUNKS, [None] * CHUNKS, [None] * CHUNKS, [None] * CHUNKS
    for h in range(CHUNKS):
        piece = lat.at[h, zh, y]
        targets = to_y if Y_FIRST[h] else to_z
        near[h] = [
            send(piece, piece, near_send.at[h, d], near_recv.at[h, d], targets[d]) for d in range(2)
        ]
        pending += near[h]

    def relay_piece(h):
        forward = h % 2 == 0
        if Y_FIRST[h]:
            return lat.at[h, zh, y_prev if forward else y_next], to_y[0 if forward else 1]
        return lat.at[h, z_prev if forward else z_next, y], to_z[0 if forward else 1]

    def group(h, which):
        if Y_FIRST[h]:
            return lat.at[h, (z_prev, zh, z_next)[which + 1]]
        return lat.at[h, :, (y_prev, y, y_next)[which + 1]]

    for step in range(CHUNKS + 3):
        h = step
        if h < CHUNKS:
            for copy in near[h]:
                copy.wait_recv()
            piece, device = relay_piece(h)
            far[h] = send(piece, piece, far_send.at[h], far_recv.at[h], device)
            pending.append(far[h])
        h = step - 1
        if 0 <= h < CHUNKS:
            far[h].wait_recv()
            targets = to_z if Y_FIRST[h] else to_y
            piece = group(h, 0)
            near2[h] = [
                send(piece, piece, near2_send.at[h, d], near2_recv.at[h, d], targets[d]) for d in range(2)
            ]
            pending += near2[h]
        h = step - 2
        if 0 <= h < CHUNKS:
            for copy in near2[h]:
                copy.wait_recv()
            targets = to_z if Y_FIRST[h] else to_y
            forward = h % 2 == 0
            piece = group(h, -1 if forward else 1)
            far2[h] = send(piece, piece, far2_send.at[h], far2_recv.at[h], targets[0 if forward else 1])
            pending.append(far2[h])
        h = step - 3
        if 0 <= h < CHUNKS:
            far2[h].wait_recv()
            if h == 0:
                for copy in w_loads:
                    copy.wait()
            block = lat[h].reshape(256, CHUNK)
            for e in range(3):
                part = lax.dot_general(
                    block, w[e, :, h * CHUNK : (h + 1) * CHUNK], (((1,), (1,)), ((), ())), preferred_element_type=F32
                )
                y_acc[e] = part if h == 0 else y_acc[e] + part

    s = lax.broadcasted_iota(jnp.int32, (1, 16, 192), 1) % 2
    first, second, third = (y_acc[e].reshape(PIECES, 16, 192) for e in range(3))
    edge = jnp.zeros((1, 16, 192), F32)
    from_left = jnp.concatenate([edge, pltpu.roll(first, 15, 1)[: PIECES - 1]], axis=0)
    from_right = jnp.concatenate([pltpu.roll(third, 1, 1)[1:], edge], axis=0)
    total = second + jnp.where(s == 1, pltpu.roll(first, 1, 1), from_left)
    total += jnp.where(s == 0, pltpu.roll(third, 15, 1), from_right)
    total = total.reshape(PIECES, 2, 8, 192)
    upper, lower = total[:, 0], total[:, 1]

    def pack(part):
        return jnp.concatenate([part[:8].reshape(64, OUT_DEV), part[8:].reshape(64, OUT_DEV)], axis=1)

    u_out[0] = pack(upper[..., 128:192])
    u_out[1] = pack(lower[..., 0:64])
    rows_sent = [
        send(u_out.at[0], u_in.at[1], u_send.at[0], u_recv.at[0], (up, col)),
        send(u_out.at[1], u_in.at[0], u_send.at[1], u_recv.at[1], (down, col)),
    ]
    load_mean.wait()
    centre = lat[col // 2, :, :, :, pl.ds(pl.multiple_of((col % 2) * CHANS, CHANS), CHANS)].reshape(256, CHANS)
    shortcut = jnp.dot(centre, g_mean[...], preferred_element_type=F32).reshape(PIECES, 2, 8, OUT_DEV)
    result0 = upper[..., 64:128] + lower[..., 128:192] + shortcut[:, 0]
    result1 = upper[..., 0:64] + lower[..., 64:128] + shortcut[:, 1]

    for copy in rows_sent:
        copy.wait_recv()

    def unpack(part, there):
        part = jnp.where(there, part, 0.0)
        return jnp.concatenate(
            [part[:, :OUT_DEV].reshape(8, 8, OUT_DEV), part[:, OUT_DEV:].reshape(8, 8, OUT_DEV)], axis=0
        )

    out_ref[0] = (result0 + unpack(u_in[0], has_up)).reshape(128, OUT_DEV).astype(BF16)
    out_ref[1] = (result1 + unpack(u_in[1], has_down)).reshape(128, OUT_DEV).astype(BF16)
    for copy in sent + pending + rows_sent:
        copy.wait_send()


def per_device(n_row, n_col, frames_in, norm_gain, first_kernel, second_kernel, latent_kernel):
    g_own, g_halo = spread_tables()
    anywhere = pl.BlockSpec(memory_space=pl.ANY)
    dma = pltpu.SemaphoreType.DMA
    out = pl.pallas_call(
        functools.partial(kernel, n_row, n_col),
        out_shape=jax.ShapeDtypeStruct((2, 128, OUT_DEV), BF16),
        in_specs=[anywhere] * 9,
        out_specs=pl.BlockSpec(memory_space=pltpu.VMEM),
        scratch_shapes=[
            pltpu.VMEM((4, 4, 16, CHANS), BF16),
            pltpu.VMEM((1, CHANS), F32),
            pltpu.VMEM((3, 3, 3, CHANS, CHANS), BF16),
            pltpu.VMEM((3, 3, 3, CHANS, CHANS), BF16),
            pltpu.VMEM((3, 3 * OUT_DEV, LATENT), BF16),
            pltpu.VMEM((1024, 256), BF16),
            pltpu.VMEM((1024, 384), BF16),
            pltpu.VMEM((128, 256), BF16),
            pltpu.VMEM((CHANS, OUT_DEV), BF16),
            pltpu.VMEM((2, 4, 16, CHANS), BF16),
            pltpu.VMEM((20, 16, CHANS), BF16),
            pltpu.VMEM((40, 16, CHANS), BF16),
            pltpu.VMEM((8, 8, 16, CHANS), BF16),
            pltpu.VMEM((6, 6, 16, CHANS), BF16),
            pltpu.VMEM((3, 576, CHANS), F32),
            pltpu.VMEM((CHUNKS, RING, RING, 16, CHUNK), BF16),
            pltpu.VMEM((3, 256, 3 * OUT_DEV), F32),
            pltpu.VMEM((2, 64, 2 * OUT_DEV), F32),
            pltpu.VMEM((2, 64, 2 * OUT_DEV), F32),
            pltpu.VMEM((256, CHANS), F32),
            dma((8,)),
            dma((9,)),
            dma((8,)),
            dma((8,)),
            dma((CHUNKS, 2)),
            dma((CHUNKS, 2)),
            dma((CHUNKS,)),
            dma((CHUNKS,)),
            dma((CHUNKS, 2)),
            dma((CHUNKS, 2)),
            dma((CHUNKS,)),
            dma((CHUNKS,)),
            dma((2,)),
            dma((2,)),
        ],
        compiler_params=pltpu.CompilerParams(
            collective_id=0, has_side_effects=True, vmem_limit_bytes=48 << 20
        ),
        cost_estimate=pl.CostEstimate(flops=4 << 30, bytes_accessed=14 << 20, transcendentals=1 << 18),
    )(
        frames_in.reshape(4, 4, 16, CHANS),
        norm_gain.reshape(1, CHANS),
        first_kernel,
        second_kernel,
        latent_kernel.transpose(0, 1, 3, 2),
        g_own,
        g_halo,
        strip_table(),
        mean_table(),
    )
    out = out.reshape(2, PIECES, FRAMES, 2, OUT_DEV)
    return out.transpose(2, 0, 1, 3, 4).reshape(FRAMES, 2, 2 * PIECES, OUT_DEV)


def solution(mesh):
    return jax.shard_map(
        functools.partial(per_device, mesh.shape["row"], mesh.shape["col"]),
        mesh=mesh,
        in_specs=(P(None, "row", "col", None), P(), P(), P(), P(None, None, None, "col")),
        out_specs=P(None, "row", None, "col"),
        check_vma=False,
    )
```

time: 182 us -> 70.8 us (0.39)
  waiting for transfers between devices: 103 us -> 0 us
  Pallas kernels: 0 us -> 61.7 us
  starting transfers between devices: 26.7 us -> 0 us
  matrix products: 18.2 us -> 0 us
  between operations: 14.2 us -> 0.02 us
  other arithmetic: 10.1 us -> 0 us
    all_gather x1 -> x0, waiting for transfers between devices: 69.1 us -> none  [per_device(): gathered = lax.all_gather(latent, 'col', axis=2, tiled=True)]
    pallas_call x0 -> x1, Pallas kernels: none -> 61.7 us  [per_device(): pl.pallas_call(functools.partial(kernel, n_row, n_col), out_shape=jax.Sha...]
    ppermute x10 -> x0, waiting for transfers between devices: 33.5 us -> none  [the longest x5 27.3 us: with_halo(): lax.ppermute(lax.slice_in_dim(block, 0, width, axis=dim), axis, backward)]
    ppermute x10 -> x0, starting transfers between devices: 26.7 us -> none  [the longest x5 17.6 us: with_halo(): lax.ppermute(lax.slice_in_dim(block, block.shape[dim] - width, None, axis...]
    dot_general x63 -> x0, matrix products: 18.2 us -> none  [the longest x54 10.1 us: conv_volume(): jnp.dot(piece, kernel[a, b, e], preferred_element_type=jnp.float32)]
    unnamed x10 -> x14, local copies, waits for them, and re-layouts: 0.03 us -> 7.43 us
    concatenate x8 -> x0, other arithmetic: 6.4 us -> none  [with_halo(): block = jnp.concatenate([low, block, high], axis=dim)]
    slice x9 -> x0, local copies, waits for them, and re-layouts: 5.45 us -> none  [the longest x1 3.15 us: per_device(): piece = padded[:, b:b + lrows, e:e + lcols].reshape(-1, width_latent)]
  transfers between devices with their start and end apart: 11 -> 0, of which waited for: 7 -> 0; matrix products, arithmetic and copies ran while one was open for 2% -> 0% of each run, Pallas kernels for 0% -> 0%
where the time goes in v1:
time: 70.8 us; the launch traced here: 69.8 us
  Pallas kernels  61.7 us (87%)
  local copies, waits for them, and re-layouts  8.11 us (11%)
    pallas_call x1, Pallas kernels, per_device(): pl.pallas_call(functools.partial(kernel, n_row, n_col), out_shape=jax.Sha...  61.7 us
    unnamed x14, local copies, waits for them, and re-layouts  7.43 us

profile of v1, /device:TPU:1, one launch (start us, length us, event | category | flops | bytes accessed | tf_op | source)
XLA Modules:
  0.0 69.8 jit_solution(8820702047937068926)
XLA Ops:
  0.0 0.0 copy-start
  0.0 2.0 %copy-done = bf16[3,3,3,256,256]{4,3,2,1,0:T(8,128)(2,1)S(1)} copy-done((bf16[3,3,3,256,256]{4,3,2,1,0:T(8,128)(2,1)S(1)}, bf16[3,3,3,256,256]{4,3,2,1,0:T(8,128)(2,1)}, u32[]{:S(2)}) %copy-start) | copy-done | bytes 3538968
  2.0 0.0 copy-start.1
  2.0 0.9 %copy-done.1 = bf16[4,8,8,256]{3,2,1,0:T(8,128)(2,1)S(1)} copy-done((bf16[4,8,8,256]{3,2,1,0:T(8,128)(2,1)S(1)}, bf16[4,8,8,256]{3,2,1,0:T(8,128)(2,1)}, u32[]{:S(2)}) %copy-start.1) | copy-done | bytes 131096
  2.9 0.0 copy-start.2
  2.9 0.7 copy-done.2
  3.6 0.0 copy-start.3
  3.6 1.1 %copy-done.3 = bf16[1024,384]{1,0:T(8,128)(2,1)S(1)} copy-done((bf16[1024,384]{1,0:T(8,128)(2,1)S(1)}, bf16[1024,384]{1,0:T(8,128)(2,1)}, u32[]{:S(2)}) %copy-start.3) | copy-done | bytes 786456
  4.7 0.0 copy-start.4
  4.7 1.0 %copy-done.4 = bf16[1024,256]{1,0:T(8,128)(2,1)S(1)} copy-done((bf16[1024,256]{1,0:T(8,128)(2,1)S(1)}, bf16[1024,256]{1,0:T(8,128)(2,1)}, u32[]{:S(2)}) %copy-start.4) | copy-done | bytes 524312
  5.8 0.0 copy-start.5
  5.8 0.8 %copy-done.5 = bf16[256,64]{1,0:T(8,128)(2,1)S(1)} copy-done((bf16[256,64]{1,0:T(8,128)(2,1)S(1)}, bf16[256,64]{1,0:T(8,128)(2,1)}, u32[]{:S(2)}) %copy-start.5) | copy-done | bytes 32792
  6.6 0.0 copy-start.6
  6.6 0.8 %copy-done.6 = bf16[128,256]{1,0:T(8,128)(2,1)S(1)} copy-done((bf16[128,256]{1,0:T(8,128)(2,1)S(1)}, bf16[128,256]{1,0:T(8,128)(2,1)}, u32[]{:S(2)}) %copy-start.6) | copy-done | bytes 65560
  7.4 61.7 %shard_map.91 = bf16[2,128,64]{2,1,0:T(8,128)(2,1)S(1)} custom-call(bf16[4,4,16,256]{3,2,1,0:T(8,128)(2,1)S(1)} %bitcast.8, f32[1,256]{1,0:T(1,128)S(1)} %bitcast.9, bf16[3,3,3,256,256]{4,3,2,1,0:T(8,128)(2,1)S(1)} %copy-done, bf16[3,3,3,256,256]{4,3,2,1,0:T(8,128)(2,1)} %k2_hbm.1, bf16[3,3,64,4096]{3,2,1,0:T(8,128)(2,1)} %bitcast.10, ...), custom_call_target="tpu_custom_call" | custom-call | flops 4294967296 | bytes 14680064 | tf_op jit(solution)/shard_map/pallas_call | solution.py:317
  69.1 0.7 copy.10
Async XLA Ops:
  0.0 2.0 %copy-start = (bf16[3,3,3,256,256]{4,3,2,1,0:T(8,128)(2,1)S(1)}, bf16[3,3,3,256,256]{4,3,2,1,0:T(8,128)(2,1)}, u32[]{:S(2)}) copy-start(bf16[3,3,3,256,256]{4,3,2,1,0:T(8,128)(2,1)} %k1_hbm.1) | copy-start | bytes 10616836
  2.0 0.9 %copy-start.1 = (bf16[4,8,8,256]{3,2,1,0:T(8,128)(2,1)S(1)}, bf16[4,8,8,256]{3,2,1,0:T(8,128)(2,1)}, u32[]{:S(2)}) copy-start(bf16[4,8,8,256]{3,2,1,0:T(8,128)(2,1)} %param.9) | copy-start | bytes 393220
  2.9 0.7 copy-start.2
  3.6 1.1 %copy-start.3 = (bf16[1024,384]{1,0:T(8,128)(2,1)S(1)}, bf16[1024,384]{1,0:T(8,128)(2,1)}, u32[]{:S(2)}) copy-start(bf16[1024,384]{1,0:T(8,128)(2,1)} %constant.9.clone.g_halo_hbm) | copy-start | bytes 2359300
  4.7 1.0 %copy-start.4 = (bf16[1024,256]{1,0:T(8,128)(2,1)S(1)}, bf16[1024,256]{1,0:T(8,128)(2,1)}, u32[]{:S(2)}) copy-start(bf16[1024,256]{1,0:T(8,128)(2,1)} %constant.8.clone.g_own_hbm) | copy-start | bytes 1572868
  5.8 0.8 %copy-start.5 = (bf16[256,64]{1,0:T(8,128)(2,1)S(1)}, bf16[256,64]{1,0:T(8,128)(2,1)}, u32[]{:S(2)}) copy-start(bf16[256,64]{1,0:T(8,128)(2,1)} %constant.11.clone.g_mean_hbm) | copy-start | bytes 98308
  6.6 0.8 %copy-start.6 = (bf16[128,256]{1,0:T(8,128)(2,1)S(1)}, bf16[128,256]{1,0:T(8,128)(2,1)}, u32[]{:S(2)}) copy-start(bf16[128,256]{1,0:T(8,128)(2,1)} %constant.10.clone.g_strip_hbm) | copy-start | bytes 196612

commit v2 on v1

--- a/solution.py
+++ b/solution.py
@@ -15,10 +15,13 @@
 OUT_CH, LATENT = 1024, 4096
 RING = 4
 PIECES = RING * RING
-CHUNKS = 8
-CHUNK = LATENT // CHUNKS
 OUT_DEV = OUT_CH // PIECES
-Y_FIRST = (False,) * CHUNKS
+PARTS = ((0, 6, False), (6, 12, False), (12, 16, True))
+CHUNKS = len(PARTS)
+ORDER = """
+    n0 n2 N00 n1 N10 f2 f0 N01 N03 f1 N11 N13 N20 N21 N23 N22
+    F00 F10 N02 N12 F01 F03 F11 F13 F20 F21 F23 F22 F02 F12 W0 W1 W2
+"""
 
 
 def one_hot(index, width):
@@ -206,69 +209,71 @@
     load_k2.wait()
     convolve(hidden, k2, 4, acc)
     mixed = (kept[...].reshape(32, 8, CHANS) + joined(acc, 256)).astype(BF16).reshape(16, 16, CHANS)
-    for tile in range(16):
-        lat[tile // 2, zh, y, :, (tile % 2) * CHANS : (tile % 2 + 1) * CHANS] = mixed[tile]
-
-    opposite_z, opposite_y = lax.rem(zh + 2, RING), lax.rem(y + 2, RING)
+    for tile in range(PIECES):
+        lat[tile, zh, y] = mixed[tile]
+
+    zs = [zh] + [lax.rem(zh + step, RING) for step in (1, 2, 3)]
+    ys = [y] + [lax.rem(y + step, RING) for step in (1, 2, 3)]
     pending = []
-    near, far, near2, far2 = [None] * CHUNKS, [None] * CHUNKS, [None] * CHUNKS, [None] * CHUNKS
-    for h in range(CHUNKS):
-        piece = lat.at[h, zh, y]
-        targets = to_y if Y_FIRST[h] else to_z
-        near[h] = [
-            send(piece, piece, near_send.at[h, d], near_recv.at[h, d], targets[d]) for d in range(2)
-        ]
-        pending += near[h]
-
-    def relay_piece(h):
-        forward = h % 2 == 0
-        if Y_FIRST[h]:
-            return lat.at[h, zh, y_prev if forward else y_next], to_y[0 if forward else 1]
-        return lat.at[h, z_prev if forward else z_next, y], to_z[0 if forward else 1]
-
-    def group(h, which):
-        if Y_FIRST[h]:
-            return lat.at[h, (z_prev, zh, z_next)[which + 1]]
-        return lat.at[h, :, (y_prev, y, y_next)[which + 1]]
-
-    for step in range(CHUNKS + 3):
-        h = step
-        if h < CHUNKS:
-            for copy in near[h]:
+    near, far, near2, far2, took = {}, {}, {}, {}, []
+
+    def pieces(c, u, v, part=None):
+        first, last, y_first = PARTS[c]
+        if part is not None:
+            middle = (first + last) // 2
+            first, last = (first, middle) if part == 0 else (middle, last)
+        a, b = (zs[v], ys[u]) if y_first else (zs[u], ys[v])
+        return lat.at[pl.ds(first, last - first), a, b]
+
+    def pass_on(piece, send_sem, recv_sem, device):
+        copy = send(piece, piece, send_sem, recv_sem, device)
+        pending.append(copy)
+        return copy
+
+    for move in ORDER.split():
+        what, c, u = move[0], int(move[1]), int(move[2:] or 0)
+        rings = (to_y, to_z) if PARTS[c][2] else (to_z, to_y)
+        if what == "n":
+            near[c] = [
+                pass_on(pieces(c, 0, 0), near_send.at[c, d], near_recv.at[c, d], rings[0][d]) for d in range(2)
+            ]
+        elif what == "f":
+            for copy in near[c]:
                 copy.wait_recv()
-            piece, device = relay_piece(h)
-            far[h] = send(piece, piece, far_send.at[h], far_recv.at[h], device)
-            pending.append(far[h])
-        h = step - 1
-        if 0 <= h < CHUNKS:
-            far[h].wait_recv()
-            targets = to_z if Y_FIRST[h] else to_y
-            piece = group(h, 0)
-            near2[h] = [
-                send(piece, piece, near2_send.at[h, d], near2_recv.at[h, d], targets[d]) for d in range(2)
+            far[c] = [
+                pass_on(pieces(c, 3 - 2 * d, 0, d), far_send.at[c, d], far_recv.at[c, d], rings[0][d]) for d in range(2)
             ]
-            pending += near2[h]
-        h = step - 2
-        if 0 <= h < CHUNKS:
-            for copy in near2[h]:
+        elif what == "N":
+            if u == 2:
+                for copy in far[c]:
+                    copy.wait_recv()
+            near2[c, u] = [
+                pass_on(pieces(c, u, 0), near2_send.at[c, u, d], near2_recv.at[c, u, d], rings[1][d]) for d in range(2)
+            ]
+        elif what == "F":
+            for copy in near2[c, u]:
                 copy.wait_recv()
-            targets = to_z if Y_FIRST[h] else to_y
-            forward = h % 2 == 0
-            piece = group(h, -1 if forward else 1)
-            far2[h] = send(piece, piece, far2_send.at[h], far2_recv.at[h], targets[0 if forward else 1])
-            pending.append(far2[h])
-        h = step - 3
-        if 0 <= h < CHUNKS:
-            far2[h].wait_recv()
-            if h == 0:
+            d = (0, 1, 1, 0)[u] if c % 2 == 0 else (1, 1, 0, 0)[u]
+            far2[c, u] = pass_on(pieces(c, u, 3 - 2 * d), far2_send.at[c, u], far2_recv.at[c, u], rings[1][d])
+        else:
+            for u in range(RING):
+                far2[c, u].wait_recv()
+            if not took:
                 for copy in w_loads:
                     copy.wait()
-            block = lat[h].reshape(256, CHUNK)
+            first, last, _ = PARTS[c]
             for e in range(3):
-                part = lax.dot_general(
-                    block, w[e, :, h * CHUNK : (h + 1) * CHUNK], (((1,), (1,)), ((), ())), preferred_element_type=F32
-                )
-                y_acc[e] = part if h == 0 else y_acc[e] + part
+                part = None if not took else y_acc[e]
+                for tile in range(first, last):
+                    term = lax.dot_general(
+                        lat[tile].reshape(256, CHANS),
+                        w[e, :, tile * CHANS : (tile + 1) * CHANS],
+                        (((1,), (1,)), ((), ())),
+                        preferred_element_type=F32,
+                    )
+                    part = term if part is None else part + term
+                y_acc[e] = part
+            took.append(c)
 
     s = lax.broadcasted_iota(jnp.int32, (1, 16, 192), 1) % 2
     first, second, third = (y_acc[e].reshape(PIECES, 16, 192) for e in range(3))
@@ -290,7 +295,7 @@
         send(u_out.at[1], u_in.at[0], u_send.at[1], u_recv.at[1], (down, col)),
     ]
     load_mean.wait()
-    centre = lat[col // 2, :, :, :, pl.ds(pl.multiple_of((col % 2) * CHANS, CHANS), CHANS)].reshape(256, CHANS)
+    centre = lat[col].reshape(256, CHANS)
     shortcut = jnp.dot(centre, g_mean[...], preferred_element_type=F32).reshape(PIECES, 2, 8, OUT_DEV)
     result0 = upper[..., 64:128] + lower[..., 128:192] + shortcut[:, 0]
     result1 = upper[..., 0:64] + lower[..., 64:128] + shortcut[:, 1]
@@ -312,7 +317,7 @@
 
 def per_device(n_row, n_col, frames_in, norm_gain, first_kernel, second_kernel, latent_kernel):
     g_own, g_halo = spread_tables()
-    anywhere = pl.BlockSpec(memory_space=pl.ANY)
+    anywhere = pl.BlockSpec(memory_space=pltpu.HBM)
     dma = pltpu.SemaphoreType.DMA
     out = pl.pallas_call(
         functools.partial(kernel, n_row, n_col),
@@ -335,7 +340,7 @@
             pltpu.VMEM((8, 8, 16, CHANS), BF16),
             pltpu.VMEM((6, 6, 16, CHANS), BF16),
             pltpu.VMEM((3, 576, CHANS), F32),
-            pltpu.VMEM((CHUNKS, RING, RING, 16, CHUNK), BF16),
+            pltpu.VMEM((PIECES, RING, RING, 16, CHANS), BF16),
             pltpu.VMEM((3, 256, 3 * OUT_DEV), F32),
             pltpu.VMEM((2, 64, 2 * OUT_DEV), F32),
             pltpu.VMEM((2, 64, 2 * OUT_DEV), F32),
@@ -346,17 +351,17 @@
             dma((8,)),
             dma((CHUNKS, 2)),
             dma((CHUNKS, 2)),
-            dma((CHUNKS,)),
-            dma((CHUNKS,)),
             dma((CHUNKS, 2)),
             dma((CHUNKS, 2)),
-            dma((CHUNKS,)),
-            dma((CHUNKS,)),
+            dma((CHUNKS, RING, 2)),
+            dma((CHUNKS, RING, 2)),
+            dma((CHUNKS, RING)),
+            dma((CHUNKS, RING)),
             dma((2,)),
             dma((2,)),
         ],
         compiler_params=pltpu.CompilerParams(
-            collective_id=0, has_side_effects=True, vmem_limit_bytes=48 << 20
+            collective_id=0, has_side_effects=True, vmem_limit_bytes=60 << 20
         ),
         cost_estimate=pl.CostEstimate(flops=4 << 30, bytes_accessed=14 << 20, transcendentals=1 << 18),
     )(

time: 70.8 us -> 50.4 us (0.71)
  the two profiles are of different devices: /device:TPU:1 before, /device:TPU:57 now
where the time goes in v2:
time: 50.4 us; the launch traced here: 50.3 us
  Pallas kernels  48.7 us (97%)
  local copies, waits for them, and re-layouts  1.52 us (3%)
    pallas_call x1, Pallas kernels, per_device(): pl.pallas_call(functools.partial(kernel, n_row, n_col), out_shape=jax.Sha...  48.7 us
    transpose x1, local copies, waits for them, and re-layouts, per_device(): return out.transpose(2, 0, 1, 3, 4).reshape(FRAMES, 2, 2 * PIECES, OUT_DEV)  1.52 us

profile of v2, /device:TPU:57, one launch (start us, length us, event | category | flops | bytes accessed | tf_op | source)
XLA Modules:
  0.0 50.3 jit_solution(2997140338090629772)
XLA Ops:
  0.0 48.7 %shard_map.91 = bf16[2,128,64]{2,1,0:T(8,128)(2,1)} custom-call(bf16[4,4,16,256]{3,2,1,0:T(8,128)(2,1)} %bitcast.9, f32[1,256]{1,0:T(1,128)} %bitcast.10, bf16[3,3,3,256,256]{4,3,2,1,0:T(8,128)(2,1)} %k1_hbm.1, bf16[3,3,3,256,256]{4,3,2,1,0:T(8,128)(2,1)} %k2_hbm.1, bf16[3,3,64,4096]{3,2,1,0:T(8,128)(2,1)} %bitcast.8, ...), custom_call_target="tpu_custom_call" | custom-call | flops 4294967296 | bytes 14680064 | tf_op jit(solution)/shard_map/pallas_call | solution.py:322
  48.8 1.5 %copy.10 = bf16[4,2,16,2,64]{4,3,2,1,0:T(2,128)(2,1)} copy(bf16[4,2,16,2,64]{4,3,0,2,1:T(2,128)(2,1)} %bitcast.7) | data formatting | bytes 65536 | tf_op jit(solution)/shard_map/transpose | solution.py:379

commit v3 on v2

--- a/solution.py
+++ b/solution.py
@@ -18,10 +18,10 @@
 OUT_DEV = OUT_CH // PIECES
 PARTS = ((0, 6, False), (6, 12, False), (12, 16, True))
 CHUNKS = len(PARTS)
-ORDER = """
-    n0 n2 N00 n1 N10 f2 f0 N01 N03 f1 N11 N13 N20 N21 N23 N22
-    F00 F10 N02 N12 F01 F03 F11 F13 F20 F21 F23 F22 F02 F12 W0 W1 W2
-"""
+ORDER = (
+    ("n0", "n2", "N00", "n1", "N10", "f2", "f0", "N01", "N03", "f1", "N11", "N13", "N20", "N21", "N23", "N22")
+    + ("F00", "F10", "N02", "N12", "F01", "F03", "F11", "F13", "F20", "F21", "F02", "F12", "F23", "F22", "W0", "W1", "W2")
+)
 
 
 def one_hot(index, width):
@@ -32,30 +32,39 @@
     return out.astype(BF16)
 
 
+OWN_TILES = [(p, q) for p in range(1, 5) for q in range(1, 5)]
+OTHER_TILES = [(p, q) for p in range(9) for q in range(9) if (p, q) not in OWN_TILES]
+
+
+def line_of(tile, half):
+    if tile < 6:
+        return 4 * half + tile - 1
+    return tile - 6 + (7 if half else -2)
+
+
 def spread_tables():
     own, halo = [], []
-    for p in range(-2, 6):
-        for q in range(-2, 6):
-            for i in range(2):
-                for f in range(FRAMES):
-                    for j in range(2):
-                        r, c = 4 * i + p, 4 * j + q
-                        inside_r, inside_c = 0 <= r < SIDE, 0 <= c < SIDE
-                        a, b = -1, -1
-                        side = 0 if c < 0 else 1
-                        cc = c + 2 if c < 0 else c - SIDE
-                        rr = r + 2 if r < 0 else r - SIDE
-                        if inside_r and inside_c:
-                            a = f * 64 + r * 8 + c
-                        elif inside_c:
-                            b = ((0 if r < 0 else 4) + f) * 16 + rr * 8 + c
-                        elif inside_r:
-                            b = (8 + 4 * side + r // 2) * 16 + f * 4 + (r % 2) * 2 + cc
-                        else:
-                            b = (16 + (0 if r < 0 else 2) + side) * 16 + f * 4 + rr * 2 + cc
-                        own.append(a)
-                        halo.append(b)
-    return one_hot(own, 256), one_hot(halo, 384)
+    for p, q in OWN_TILES + OTHER_TILES:
+        for i in range(2):
+            for f in range(FRAMES):
+                for j in range(2):
+                    r, c = line_of(p, i), line_of(q, j)
+                    inside_r, inside_c = 0 <= r < SIDE, 0 <= c < SIDE
+                    a, b = -1, -1
+                    side = 0 if c < 0 else 1
+                    cc = c + 2 if c < 0 else c - SIDE
+                    rr = r + 2 if r < 0 else r - SIDE
+                    if inside_r and inside_c:
+                        a = f * 64 + r * 8 + c
+                    elif inside_c:
+                        b = ((0 if r < 0 else 4) + f) * 16 + rr * 8 + c
+                    elif inside_r:
+                        b = (8 + 4 * side + r // 2) * 16 + f * 4 + (r % 2) * 2 + cc
+                    else:
+                        b = (16 + (0 if r < 0 else 2) + side) * 16 + f * 4 + rr * 2 + cc
+                    own.append(a)
+                    halo.append(b)
+    return one_hot(own, 256), one_hot(halo[256:], 384)
 
 
 def strip_table():
@@ -76,21 +85,56 @@
     return out.astype(BF16)
 
 
-def convolve(src, w, n, acc):
-    rows = n * n * 16
+def convolve_own(cells, w, acc):
+    order = [(1, 1)] + [(b, e) for b in range(3) for e in range(3) if (b, e) != (1, 1)]
+    for a in range(3):
+        for b, e in order:
+            p0, p1, q0, q1 = max(0, 1 - b), min(4, 5 - b), max(0, 1 - e), min(4, 5 - e)
+            shape = (p1 - p0, q1 - q0, 16, CHANS)
+            lhs = cells[p0 + b : p1 + b, q0 + e : q1 + e].reshape(-1, CHANS)
+            part = jnp.dot(lhs, w[a, b, e], preferred_element_type=F32).reshape(shape)
+            if (b, e) == (1, 1):
+                acc[a, 0:4, 0:4] = part
+            else:
+                acc[a, p0:p1, q0:q1] += part
+
+
+def convolve_rest(cells, w, acc):
+    for a in range(3):
+        for b in range(3):
+            for e in range(3):
+                tiles = [
+                    (p, q) for p in range(5) for q in range(5)
+                    if p == 4 or q == 4 or not (1 <= p + b <= 4 and 1 <= q + e <= 4)
+                ]
+                lhs = jnp.concatenate(
+                    [cells[p + b if p < 4 else 6 + b, q + e if q < 4 else 6 + e] for p, q in tiles], axis=0
+                )
+                part = jnp.dot(lhs, w[a, b, e], preferred_element_type=F32)
+                for at, (p, q) in enumerate(tiles):
+                    term = part[at * 16 : (at + 1) * 16]
+                    if (p == 4 or q == 4) and b == 0 and e == 0:
+                        acc[a, p, q] = term
+                    else:
+                        acc[a, p, q] += term
+
+
+def convolve(src, w, acc):
     for a in range(3):
         total = None
         for b in range(3):
             for e in range(3):
-                part = jnp.dot(src[b : b + n, e : e + n].reshape(rows, CHANS), w[a, b, e], preferred_element_type=F32)
+                part = jnp.dot(src[b : b + 4, e : e + 4].reshape(256, CHANS), w[a, b, e], preferred_element_type=F32)
                 total = part if total is None else total + part
-        acc[a, :rows] = total
-
-
-def joined(acc, rows):
-    early, same, late = (acc[a, :rows].reshape(rows // 8, 8, CHANS) for a in range(3))
+        acc[a, 0:4, 0:4] = total.reshape(4, 4, 16, CHANS)
+
+
+def joined(acc, n):
+    early, same, late = (acc[a, 0:n, 0:n].reshape(n * n * 2, 8, CHANS) for a in range(3))
     f = lax.broadcasted_iota(jnp.int32, (1, 8, CHANS), 1) // 2
-    return same + jnp.where(f > 0, pltpu.roll(early, 2, 1), 0.0) + jnp.where(f < FRAMES - 1, pltpu.roll(late, 6, 1), 0.0)
+    total = same + jnp.where(f > 0, pltpu.roll(early, 2, 1), 0.0)
+    total += jnp.where(f < FRAMES - 1, pltpu.roll(late, 6, 1), 0.0)
+    return total.reshape(n, n, 2, 8, CHANS)
 
 
 def kernel(
@@ -98,7 +142,7 @@
     x_hbm, gain_hbm, k1_hbm, k2_hbm, w_hbm, g_own_hbm, g_halo_hbm, g_strip_hbm, g_mean_hbm,
     out_ref,
     x, gain, k1, k2, w, g_own, g_halo, g_strip, g_mean,
-    strips, halo, normed, cells, hidden, acc, lat, y_acc, u_out, u_in, kept,
+    strips, halo, normed, cells, others, hidden, acc, lat, y_acc, u_out, u_in, kept,
     load_sem, w_sem, halo_send, halo_recv,
     near_send, near_recv, far_send, far_recv, near2_send, near2_recv, far2_send, far2_recv,
     u_send, u_recv,
@@ -122,8 +166,8 @@
 
     loads = []
     for at, (source, target) in enumerate((
-        (x_hbm, x), (g_strip_hbm, g_strip), (gain_hbm, gain), (g_own_hbm, g_own), (g_halo_hbm, g_halo),
-        (k1_hbm, k1), (k2_hbm, k2), (g_mean_hbm, g_mean),
+        (x_hbm, x), (g_strip_hbm, g_strip), (gain_hbm, gain), (g_own_hbm, g_own), (k1_hbm, k1),
+        (g_halo_hbm, g_halo), (k2_hbm, k2), (g_mean_hbm, g_mean),
     )):
         copy = pltpu.make_async_copy(source, target, load_sem.at[at])
         copy.start()
@@ -134,7 +178,7 @@
             copy = pltpu.make_async_copy(w_hbm.at[b, e], w.at[e, pl.ds(b * OUT_DEV, OUT_DEV)], w_sem.at[b * 3 + e])
             copy.start()
             w_loads.append(copy)
-    load_x, load_strip, load_gain, load_own, load_halo, load_k1, load_k2, load_mean = loads
+    load_x, load_strip, load_gain, load_own, load_k1, load_halo, load_k2, load_mean = loads
 
     def send(source, target, send_sem, recv_sem, device):
         copy = pltpu.make_async_remote_copy(
@@ -144,19 +188,17 @@
         return copy
 
     load_x.wait()
-    pl.semaphore_wait(barrier, len(around))
-    sent = [
-        send(x.at[:, 0], halo.at[pl.ds(4, 4)], halo_send.at[0], halo_recv.at[0], (up, col)),
-        send(x.at[:, 3], halo.at[pl.ds(0, 4)], halo_send.at[1], halo_recv.at[1], (down, col)),
-    ]
     load_strip.wait()
     own = x[...].reshape(256, CHANS)
     strips[...] = jnp.dot(g_strip[...], own, preferred_element_type=F32).astype(BF16).reshape(2, 4, 16, CHANS)
-    sent += [
+    pl.semaphore_wait(barrier, len(around))
+    sent = [
         send(strips.at[0, 3], halo.at[17], halo_send.at[4], halo_recv.at[4], (down, left)),
         send(strips.at[1, 3], halo.at[16], halo_send.at[5], halo_recv.at[5], (down, right)),
         send(strips.at[0, 0], halo.at[19], halo_send.at[6], halo_recv.at[6], (up, left)),
         send(strips.at[1, 0], halo.at[18], halo_send.at[7], halo_recv.at[7], (up, right)),
+        send(x.at[:, 0], halo.at[pl.ds(4, 4)], halo_send.at[0], halo_recv.at[0], (up, col)),
+        send(x.at[:, 3], halo.at[pl.ds(0, 4)], halo_send.at[1], halo_recv.at[1], (down, col)),
         send(strips.at[0], halo.at[pl.ds(12, 4)], halo_send.at[2], halo_recv.at[2], (row, left)),
         send(strips.at[1], halo.at[pl.ds(8, 4)], halo_send.at[3], halo_recv.at[3], (row, right)),
     ]
@@ -168,11 +210,16 @@
         scale = lax.rsqrt(jnp.mean(values * values, axis=-1, keepdims=True) + 1e-06)
         return values * scale * gain[...]
 
-    normed[0:16] = norm(own).astype(BF16).reshape(16, 16, CHANS)
-    normed[36:40] = jnp.zeros((4, 16, CHANS), BF16)
+    own_normed = norm(own).astype(BF16)
+    normed[20:24] = jnp.zeros((4, 16, CHANS), BF16)
     load_own.wait()
-    middle = g_own[...].reshape(8, 8, 16, 256)[2:6, 2:6].reshape(256, 256)
-    kept[...] = jnp.dot(middle, own, preferred_element_type=F32)
+    middle = jnp.dot(g_own[0:256], own_normed, preferred_element_type=F32)
+    cells[1:5, 1:5] = middle.astype(BF16).reshape(4, 4, 16, CHANS)
+    load_k1.wait()
+    convolve_own(cells, k1, acc)
+    others[...] = jnp.dot(g_own[256:], own_normed, preferred_element_type=F32)
+    kept[...] = jnp.dot(g_own[0:256], own, preferred_element_type=F32)
+    load_halo.wait()
 
     for copy in sent:
         copy.wait_recv()
@@ -185,30 +232,32 @@
     ):
         values = norm(halo[start : start + count].reshape(count * 16, CHANS))
         values = values * jnp.where(there, 1.0, 0.0).astype(F32)
-        normed[16 + start : 16 + start + count] = values.astype(BF16).reshape(count, 16, CHANS)
-    load_halo.wait()
-    spread = jnp.dot(g_own[...], normed[0:16].reshape(256, CHANS), preferred_element_type=F32)
-    spread += jnp.dot(g_halo[...], normed[16:40].reshape(384, CHANS), preferred_element_type=F32)
-    cells[...] = spread.astype(BF16).reshape(8, 8, 16, CHANS)
-
-    load_k1.wait()
-    convolve(cells, k1, 6, acc)
-    value = joined(acc, 576)
-    value = (value / (1.0 + jnp.exp(-value))).reshape(6, 6, 2, 8, CHANS)
-    hidden[...] = value.astype(BF16).reshape(6, 6, 16, CHANS)
-    place = lax.broadcasted_iota(jnp.int32, (1, 16, CHANS), 1)
-    i_of, j_of = place // 8, place % 2
-    none = jnp.zeros((), BF16)
-    for edge, outside, there in ((0, i_of == 0, has_up), (5, i_of == 1, has_down)):
-        keep = jnp.logical_or(jnp.logical_not(outside), there)
-        hidden[edge] = jnp.where(keep, hidden[edge].astype(F32), 0.0).astype(BF16)
-    for edge, outside, there in ((0, j_of == 0, has_left), (5, j_of == 1, has_right)):
-        keep = jnp.logical_or(jnp.logical_not(outside), there)
-        hidden[:, edge] = jnp.where(keep, hidden[:, edge].astype(F32), 0.0).astype(BF16)
+        normed[start : start + count] = values.astype(BF16).reshape(count, 16, CHANS)
+    spread = others[...] + jnp.dot(g_halo[...], normed[...].reshape(384, CHANS), preferred_element_type=F32)
+    for at, (p, q) in enumerate(OTHER_TILES):
+        cells[p, q] = spread[at * 16 : (at + 1) * 16].astype(BF16)
+
+    convolve_rest(cells, k1, acc)
+    value = joined(acc, 5)
+    value = value / (1.0 + jnp.exp(-value))
+    def flag(there):
+        return jnp.where(there, 1.0, 0.0).astype(F32)
+
+    j_of = lax.broadcasted_iota(jnp.int32, (1, 8, CHANS), 1) % 2
+    sides = jnp.where(j_of == 0, flag(has_left), flag(has_right))
+    inner, below = value[0:4], value[4]
+    top = jnp.stack([below[:, 0] * flag(has_up), inner[3][:, 0]], axis=1)
+    bottom = jnp.stack([inner[0][:, 1], below[:, 1] * flag(has_down)], axis=1)
+    for p, line in enumerate((top, inner[0], inner[1], inner[2], inner[3], bottom)):
+        edge = line[4] * sides
+        first = jnp.where(j_of == 0, edge, pltpu.roll(line[3], 1, 1))
+        last = jnp.where(j_of == 1, edge, pltpu.roll(line[0], 7, 1))
+        for q, tile in enumerate((first, line[0], line[1], line[2], line[3], last)):
+            hidden[p, q] = tile.reshape(16, CHANS).astype(BF16)
 
     load_k2.wait()
-    convolve(hidden, k2, 4, acc)
-    mixed = (kept[...].reshape(32, 8, CHANS) + joined(acc, 256)).astype(BF16).reshape(16, 16, CHANS)
+    convolve(hidden, k2, acc)
+    mixed = (kept[...].reshape(4, 4, 2, 8, CHANS) + joined(acc, 4)).astype(BF16).reshape(16, 16, CHANS)
     for tile in range(PIECES):
         lat[tile, zh, y] = mixed[tile]
 
@@ -230,7 +279,7 @@
         pending.append(copy)
         return copy
 
-    for move in ORDER.split():
+    for move in ORDER:
         what, c, u = move[0], int(move[1]), int(move[2:] or 0)
         rings = (to_y, to_z) if PARTS[c][2] else (to_z, to_y)
         if what == "n":
@@ -330,16 +379,17 @@
             pltpu.VMEM((3, 3, 3, CHANS, CHANS), BF16),
             pltpu.VMEM((3, 3, 3, CHANS, CHANS), BF16),
             pltpu.VMEM((3, 3 * OUT_DEV, LATENT), BF16),
-            pltpu.VMEM((1024, 256), BF16),
-            pltpu.VMEM((1024, 384), BF16),
+            pltpu.VMEM((81 * 16, 256), BF16),
+            pltpu.VMEM((65 * 16, 384), BF16),
             pltpu.VMEM((128, 256), BF16),
             pltpu.VMEM((CHANS, OUT_DEV), BF16),
             pltpu.VMEM((2, 4, 16, CHANS), BF16),
             pltpu.VMEM((20, 16, CHANS), BF16),
-            pltpu.VMEM((40, 16, CHANS), BF16),
-            pltpu.VMEM((8, 8, 16, CHANS), BF16),
+            pltpu.VMEM((24, 16, CHANS), BF16),
+            pltpu.VMEM((9, 9, 16, CHANS), BF16),
+            pltpu.VMEM((65 * 16, CHANS), F32),
             pltpu.VMEM((6, 6, 16, CHANS), BF16),
-            pltpu.VMEM((3, 576, CHANS), F32),
+            pltpu.VMEM((3, 5, 5, 16, CHANS), F32),
             pltpu.VMEM((PIECES, RING, RING, 16, CHANS), BF16),
             pltpu.VMEM((3, 256, 3 * OUT_DEV), F32),
             pltpu.VMEM((2, 64, 2 * OUT_DEV), F32),

time: 50.4 us -> 48.4 us (0.960)
  the two profiles are of different devices: /device:TPU:57 before, /device:TPU:1 now
where the time goes in v3:
time: 48.4 us; the launch traced here: 47.6 us
  Pallas kernels  46.1 us (95%)
  local copies, waits for them, and re-layouts  1.52 us (3%)
    pallas_call x1, Pallas kernels, per_device(): pl.pallas_call(functools.partial(kernel, n_row, n_col), out_shape=jax.Sha...  46.1 us
    transpose x1, local copies, waits for them, and re-layouts, per_device(): return out.transpose(2, 0, 1, 3, 4).reshape(FRAMES, 2, 2 * PIECES, OUT_DEV)  1.52 us

profile of v3, /device:TPU:1, one launch (start us, length us, event | category | flops | bytes accessed | tf_op | source)
XLA Modules:
  0.0 47.6 jit_solution(12921126762074582116)
XLA Ops:
  0.0 46.1 %shard_map.91 = bf16[2,128,64]{2,1,0:T(8,128)(2,1)} custom-call(bf16[4,4,16,256]{3,2,1,0:T(8,128)(2,1)} %bitcast.9, f32[1,256]{1,0:T(1,128)} %bitcast.10, bf16[3,3,3,256,256]{4,3,2,1,0:T(8,128)(2,1)} %k1_hbm.1, bf16[3,3,3,256,256]{4,3,2,1,0:T(8,128)(2,1)} %k2_hbm.1, bf16[3,3,64,4096]{3,2,1,0:T(8,128)(2,1)} %bitcast.8, ...), custom_call_target="tpu_custom_call" | custom-call | flops 4294967296 | bytes 14680064 | tf_op jit(solution)/shard_map/pallas_call | solution.py:371
  46.1 1.5 %copy.10 = bf16[4,2,16,2,64]{4,3,2,1,0:T(2,128)(2,1)} copy(bf16[4,2,16,2,64]{4,3,0,2,1:T(2,128)(2,1)} %bitcast.7) | data formatting | bytes 65536 | tf_op jit(solution)/shard_map/transpose | solution.py:429

commit v4 on v3

--- a/solution.py
+++ b/solution.py
@@ -19,8 +19,8 @@
 PARTS = ((0, 6, False), (6, 12, False), (12, 16, True))
 CHUNKS = len(PARTS)
 ORDER = (
-    ("n0", "n2", "N00", "n1", "N10", "f2", "f0", "N01", "N03", "f1", "N11", "N13", "N20", "N21", "N23", "N22")
-    + ("F00", "F10", "N02", "N12", "F01", "F03", "F11", "F13", "F20", "F21", "F02", "F12", "F23", "F22", "W0", "W1", "W2")
+    ("C0", "C1", "n0", "n2", "d2", "N00", "n1", "N10", "e2", "f0", "N01", "N03", "f1", "N11", "N13", "N20", "N21", "N23", "N22")
+    + ("F00", "F10", "D02", "D12", "F01", "F03", "F11", "F13", "F20", "F21", "F23", "F22", "W00132", "W10132", "W20132")
 )
 
 
@@ -119,22 +119,23 @@
                         acc[a, p, q] += term
 
 
-def convolve(src, w, acc):
+def convolve(src, w, acc, half):
     for a in range(3):
         total = None
         for b in range(3):
             for e in range(3):
-                part = jnp.dot(src[b : b + 4, e : e + 4].reshape(256, CHANS), w[a, b, e], preferred_element_type=F32)
+                lhs = src[2 * half + b : 2 * half + b + 2, e : e + 4].reshape(128, CHANS)
+                part = jnp.dot(lhs, w[a, b, e], preferred_element_type=F32)
                 total = part if total is None else total + part
-        acc[a, 0:4, 0:4] = total.reshape(4, 4, 16, CHANS)
-
-
-def joined(acc, n):
-    early, same, late = (acc[a, 0:n, 0:n].reshape(n * n * 2, 8, CHANS) for a in range(3))
+        acc[a, 0:2, 0:4] = total.reshape(2, 4, 16, CHANS)
+
+
+def joined(acc, m, n):
+    early, same, late = (acc[a, 0:m, 0:n].reshape(m * n * 2, 8, CHANS) for a in range(3))
     f = lax.broadcasted_iota(jnp.int32, (1, 8, CHANS), 1) // 2
     total = same + jnp.where(f > 0, pltpu.roll(early, 2, 1), 0.0)
     total += jnp.where(f < FRAMES - 1, pltpu.roll(late, 6, 1), 0.0)
-    return total.reshape(n, n, 2, 8, CHANS)
+    return total.reshape(m, n, 2, 8, CHANS)
 
 
 def kernel(
@@ -156,11 +157,14 @@
     to_z = ((row, z_next * RING + y), (row, z_prev * RING + y))
     to_y = ((row, zh * RING + y_next), (row, zh * RING + y_prev))
 
+    to_z2 = (row, lax.rem(zh + 2, RING) * RING + y)
+    to_y2 = (row, zh * RING + lax.rem(y + 2, RING))
+
     barrier = pltpu.get_barrier_semaphore()
     around = (
         (up, col), (down, col), (row, left), (row, right),
         (up, left), (up, right), (down, left), (down, right),
-    ) + to_z + to_y
+    ) + to_z + to_y + (to_z2, to_y2)
     for target in around:
         pl.semaphore_signal(barrier, inc=1, device_id=target, device_id_type=MESH)
 
@@ -174,10 +178,9 @@
         loads.append(copy)
     w_loads = []
     for b in range(3):
-        for e in range(3):
-            copy = pltpu.make_async_copy(w_hbm.at[b, e], w.at[e, pl.ds(b * OUT_DEV, OUT_DEV)], w_sem.at[b * 3 + e])
-            copy.start()
-            w_loads.append(copy)
+        copy = pltpu.make_async_copy(w_hbm.at[b], w.at[b], w_sem.at[b])
+        copy.start()
+        w_loads.append(copy)
     load_x, load_strip, load_gain, load_own, load_k1, load_halo, load_k2, load_mean = loads
 
     def send(source, target, send_sem, recv_sem, device):
@@ -212,6 +215,7 @@
 
     own_normed = norm(own).astype(BF16)
     normed[20:24] = jnp.zeros((4, 16, CHANS), BF16)
+    y_acc[...] = jnp.zeros(y_acc.shape, F32)
     load_own.wait()
     middle = jnp.dot(g_own[0:256], own_normed, preferred_element_type=F32)
     cells[1:5, 1:5] = middle.astype(BF16).reshape(4, 4, 16, CHANS)
@@ -238,7 +242,7 @@
         cells[p, q] = spread[at * 16 : (at + 1) * 16].astype(BF16)
 
     convolve_rest(cells, k1, acc)
-    value = joined(acc, 5)
+    value = joined(acc, 5, 5)
     value = value / (1.0 + jnp.exp(-value))
     def flag(there):
         return jnp.where(there, 1.0, 0.0).astype(F32)
@@ -256,15 +260,18 @@
             hidden[p, q] = tile.reshape(16, CHANS).astype(BF16)
 
     load_k2.wait()
-    convolve(hidden, k2, acc)
-    mixed = (kept[...].reshape(4, 4, 2, 8, CHANS) + joined(acc, 4)).astype(BF16).reshape(16, 16, CHANS)
-    for tile in range(PIECES):
-        lat[tile, zh, y] = mixed[tile]
+
+    def mix(half):
+        convolve(hidden, k2, acc, half)
+        before = kept[128 * half : 128 * half + 128].reshape(2, 4, 2, 8, CHANS)
+        mixed = (before + joined(acc, 2, 4)).astype(BF16).reshape(8, 16, CHANS)
+        for tile in range(8):
+            lat[8 * half + tile, zh, y] = mixed[tile]
 
     zs = [zh] + [lax.rem(zh + step, RING) for step in (1, 2, 3)]
     ys = [y] + [lax.rem(y + step, RING) for step in (1, 2, 3)]
     pending = []
-    near, far, near2, far2, took = {}, {}, {}, {}, []
+    near, far, near2, far2 = {}, {}, {}, {}
 
     def pieces(c, u, v, part=None):
         first, last, y_first = PARTS[c]
@@ -274,14 +281,43 @@
         a, b = (zs[v], ys[u]) if y_first else (zs[u], ys[v])
         return lat.at[pl.ds(first, last - first), a, b]
 
+    def straight(c, u):
+        return any(move == "D%d%d" % (c, u) for move in ORDER)
+
     def pass_on(piece, send_sem, recv_sem, device):
         copy = send(piece, piece, send_sem, recv_sem, device)
         pending.append(copy)
         return copy
 
+    def multiply(c, which, taps):
+        first, last, y_first = PARTS[c]
+        for b in taps:
+            part = None
+            for tile in range(first, last):
+                block = jnp.concatenate(
+                    [(lat[tile, :, ys[u]] if y_first else lat[tile, zs[u]]).reshape(64, CHANS) for u in which], axis=0
+                )
+                term = lax.dot_general(
+                    block,
+                    w[b, :, tile * CHANS : (tile + 1) * CHANS],
+                    (((1,), (1,)), ((), ())),
+                    preferred_element_type=F32,
+                )
+                part = term if part is None else part + term
+            for at, u in enumerate(which):
+                term = part[at * 64 : (at + 1) * 64].reshape(RING, 16, 3 * OUT_DEV)
+                if y_first:
+                    y_acc[b, :, ys[u]] += term
+                else:
+                    y_acc[b, zs[u]] += term
+
     for move in ORDER:
-        what, c, u = move[0], int(move[1]), int(move[2:] or 0)
+        what, c, u = move[0], int(move[1]), int(move[2:3] or 0)
+        if what == "C":
+            mix(c)
+            continue
         rings = (to_y, to_z) if PARTS[c][2] else (to_z, to_y)
+        opposite = (to_y2, to_z2) if PARTS[c][2] else (to_z2, to_y2)
         if what == "n":
             near[c] = [
                 pass_on(pieces(c, 0, 0), near_send.at[c, d], near_recv.at[c, d], rings[0][d]) for d in range(2)
@@ -292,62 +328,68 @@
             far[c] = [
                 pass_on(pieces(c, 3 - 2 * d, 0, d), far_send.at[c, d], far_recv.at[c, d], rings[0][d]) for d in range(2)
             ]
-        elif what == "N":
+        elif what == "d":
+            far[c] = [pass_on(pieces(c, 0, 0), far_send.at[c, 0], far_recv.at[c, 0], opposite[0])]
+        elif what == "e":
+            for copy in near[c]:
+                copy.wait_recv()
+        elif what in "ND":
             if u == 2:
                 for copy in far[c]:
                     copy.wait_recv()
             near2[c, u] = [
                 pass_on(pieces(c, u, 0), near2_send.at[c, u, d], near2_recv.at[c, u, d], rings[1][d]) for d in range(2)
             ]
+            if what == "D":
+                far2[c, u] = pass_on(pieces(c, u, 0), far2_send.at[c, u], far2_recv.at[c, u], opposite[1])
         elif what == "F":
             for copy in near2[c, u]:
                 copy.wait_recv()
             d = (0, 1, 1, 0)[u] if c % 2 == 0 else (1, 1, 0, 0)[u]
             far2[c, u] = pass_on(pieces(c, u, 3 - 2 * d), far2_send.at[c, u], far2_recv.at[c, u], rings[1][d])
         else:
-            for u in range(RING):
+            for copy in w_loads:
+                copy.wait()
+            w_loads = []
+            which = [int(u) for u in move[2:]]
+            for u in which:
+                if straight(c, u):
+                    for copy in near2[c, u]:
+                        copy.wait_recv()
                 far2[c, u].wait_recv()
-            if not took:
-                for copy in w_loads:
-                    copy.wait()
-            first, last, _ = PARTS[c]
-            for e in range(3):
-                part = None if not took else y_acc[e]
-                for tile in range(first, last):
-                    term = lax.dot_general(
-                        lat[tile].reshape(256, CHANS),
-                        w[e, :, tile * CHANS : (tile + 1) * CHANS],
-                        (((1,), (1,)), ((), ())),
-                        preferred_element_type=F32,
-                    )
-                    part = term if part is None else part + term
-                y_acc[e] = part
-            took.append(c)
-
-    s = lax.broadcasted_iota(jnp.int32, (1, 16, 192), 1) % 2
-    first, second, third = (y_acc[e].reshape(PIECES, 16, 192) for e in range(3))
-    edge = jnp.zeros((1, 16, 192), F32)
-    from_left = jnp.concatenate([edge, pltpu.roll(first, 15, 1)[: PIECES - 1]], axis=0)
-    from_right = jnp.concatenate([pltpu.roll(third, 1, 1)[1:], edge], axis=0)
-    total = second + jnp.where(s == 1, pltpu.roll(first, 1, 1), from_left)
-    total += jnp.where(s == 0, pltpu.roll(third, 15, 1), from_right)
-    total = total.reshape(PIECES, 2, 8, 192)
-    upper, lower = total[:, 0], total[:, 1]
+            if move != ORDER[-1]:
+                multiply(c, which, range(3))
+
+    s = lax.broadcasted_iota(jnp.int32, (1, 16, OUT_DEV), 1) % 2
+    edge = jnp.zeros((1, 16, OUT_DEV), F32)
+
+    def moved(b):
+        sums = y_acc[b].reshape(PIECES, 16, 3 * OUT_DEV)
+        first, second, third = (sums[..., e * OUT_DEV : (e + 1) * OUT_DEV] for e in range(3))
+        from_left = jnp.concatenate([edge, pltpu.roll(first, 15, 1)[: PIECES - 1]], axis=0)
+        from_right = jnp.concatenate([pltpu.roll(third, 1, 1)[1:], edge], axis=0)
+        total = second + jnp.where(s == 1, pltpu.roll(first, 1, 1), from_left)
+        total += jnp.where(s == 0, pltpu.roll(third, 15, 1), from_right)
+        return total.reshape(PIECES, 2, 8, OUT_DEV)
 
     def pack(part):
         return jnp.concatenate([part[:8].reshape(64, OUT_DEV), part[8:].reshape(64, OUT_DEV)], axis=1)
 
-    u_out[0] = pack(upper[..., 128:192])
-    u_out[1] = pack(lower[..., 0:64])
+    multiply(c, which, (0, 2))
+    above, below = moved(0), moved(2)
+    u_out[0] = pack(below[:, 0])
+    u_out[1] = pack(above[:, 1])
     rows_sent = [
         send(u_out.at[0], u_in.at[1], u_send.at[0], u_recv.at[0], (up, col)),
         send(u_out.at[1], u_in.at[0], u_send.at[1], u_recv.at[1], (down, col)),
     ]
+    multiply(c, which, (1,))
     load_mean.wait()
     centre = lat[col].reshape(256, CHANS)
     shortcut = jnp.dot(centre, g_mean[...], preferred_element_type=F32).reshape(PIECES, 2, 8, OUT_DEV)
-    result0 = upper[..., 64:128] + lower[..., 128:192] + shortcut[:, 0]
-    result1 = upper[..., 0:64] + lower[..., 64:128] + shortcut[:, 1]
+    same = moved(1) + shortcut
+    result0 = same[:, 0] + below[:, 1]
+    result1 = same[:, 1] + above[:, 0]
 
     for copy in rows_sent:
         copy.wait_recv()
@@ -391,12 +433,12 @@
             pltpu.VMEM((6, 6, 16, CHANS), BF16),
             pltpu.VMEM((3, 5, 5, 16, CHANS), F32),
             pltpu.VMEM((PIECES, RING, RING, 16, CHANS), BF16),
-            pltpu.VMEM((3, 256, 3 * OUT_DEV), F32),
+            pltpu.VMEM((3, RING, RING, 16, 3 * OUT_DEV), F32),
             pltpu.VMEM((2, 64, 2 * OUT_DEV), F32),
             pltpu.VMEM((2, 64, 2 * OUT_DEV), F32),
             pltpu.VMEM((256, CHANS), F32),
             dma((8,)),
-            dma((9,)),
+            dma((3,)),
             dma((8,)),
             dma((8,)),
             dma((CHUNKS, 2)),
@@ -419,7 +461,7 @@
         norm_gain.reshape(1, CHANS),
         first_kernel,
         second_kernel,
-        latent_kernel.transpose(0, 1, 3, 2),
+        latent_kernel.transpose(0, 1, 3, 2).reshape(3, 3 * OUT_DEV, LATENT),
         g_own,
         g_halo,
         strip_table(),

time: 48.4 us -> 47 us (0.971); the launches traced: 47.6 us -> 46.8 us
  Pallas kernels: 46.1 us -> 45.3 us
    pallas_call x1, Pallas kernels: 46.1 us -> 45.3 us  [per_device(): pl.pallas_call(functools.partial(kernel, n_row, n_col), out_shape=jax.Sha...]
where the time goes in v4:
time: 47 us; the launch traced here: 46.8 us
  Pallas kernels  45.3 us (96%)
  local copies, waits for them, and re-layouts  1.52 us (3%)
    pallas_call x1, Pallas kernels, per_device(): pl.pallas_call(functools.partial(kernel, n_row, n_col), out_shape=jax.Sha...  45.3 us
    transpose x1, local copies, waits for them, and re-layouts, per_device(): return out.transpose(2, 0, 1, 3, 4).reshape(FRAMES, 2, 2 * PIECES, OUT_DEV)  1.52 us

profile of v4, /device:TPU:1, one launch (start us, length us, event | category | flops | bytes accessed | tf_op | source)
XLA Modules:
  0.0 46.8 jit_solution(11808795549934849317)
XLA Ops:
  0.0 45.3 %shard_map.91 = bf16[2,128,64]{2,1,0:T(8,128)(2,1)} custom-call(bf16[4,4,16,256]{3,2,1,0:T(8,128)(2,1)} %bitcast.11, f32[1,256]{1,0:T(1,128)} %bitcast.12, bf16[3,3,3,256,256]{4,3,2,1,0:T(8,128)(2,1)} %k1_hbm.1, bf16[3,3,3,256,256]{4,3,2,1,0:T(8,128)(2,1)} %k2_hbm.1, bf16[3,192,4096]{2,1,0:T(8,128)(2,1)} %bitcast.10, ...), custom_call_target="tpu_custom_call" | custom-call | flops 4294967296 | bytes 14680064 | tf_op jit(solution)/shard_map/pallas_call | solution.py:413
  45.3 1.5 %copy.10 = bf16[4,2,16,2,64]{4,3,2,1,0:T(2,128)(2,1)} copy(bf16[4,2,16,2,64]{4,3,0,2,1:T(2,128)(2,1)} %bitcast.9) | data formatting | bytes 65536 | tf_op jit(solution)/shard_map/transpose | solution.py:471

commit v5 on v4

--- a/solution.py
+++ b/solution.py
@@ -33,7 +33,8 @@
 
 
 OWN_TILES = [(p, q) for p in range(1, 5) for q in range(1, 5)]
-OTHER_TILES = [(p, q) for p in range(9) for q in range(9) if (p, q) not in OWN_TILES]
+CORNER_TILES = [(p, q) for p in (0, 5, 6, 7, 8) for q in (0, 5, 6, 7, 8)]
+SIDE_TILES = [(p, q) for p in range(9) for q in range(9) if (p, q) not in OWN_TILES + CORNER_TILES]
 
 
 def line_of(tile, half):
@@ -44,7 +45,7 @@
 
 def spread_tables():
     own, halo = [], []
-    for p, q in OWN_TILES + OTHER_TILES:
+    for p, q in OWN_TILES + SIDE_TILES + CORNER_TILES:
         for i in range(2):
             for f in range(FRAMES):
                 for j in range(2):
@@ -86,6 +87,8 @@
 
 
 def convolve_own(cells, w, acc):
+    acc[:, 4] = jnp.zeros((3, 5, 16, CHANS), F32)
+    acc[:, 0:4, 4] = jnp.zeros((3, 4, 16, CHANS), F32)
     order = [(1, 1)] + [(b, e) for b in range(3) for e in range(3) if (b, e) != (1, 1)]
     for a in range(3):
         for b, e in order:
@@ -99,24 +102,18 @@
                 acc[a, p0:p1, q0:q1] += part
 
 
-def convolve_rest(cells, w, acc):
+def convolve_rest(cells, w, acc, sources):
     for a in range(3):
         for b in range(3):
             for e in range(3):
-                tiles = [
-                    (p, q) for p in range(5) for q in range(5)
-                    if p == 4 or q == 4 or not (1 <= p + b <= 4 and 1 <= q + e <= 4)
-                ]
-                lhs = jnp.concatenate(
-                    [cells[p + b if p < 4 else 6 + b, q + e if q < 4 else 6 + e] for p, q in tiles], axis=0
-                )
+                reads = {
+                    (p, q): (p + b if p < 4 else 6 + b, q + e if q < 4 else 6 + e) for p in range(5) for q in range(5)
+                }
+                tiles = [tile for tile in reads if reads[tile] in sources]
+                lhs = jnp.concatenate([cells[reads[tile]] for tile in tiles], axis=0)
                 part = jnp.dot(lhs, w[a, b, e], preferred_element_type=F32)
                 for at, (p, q) in enumerate(tiles):
-                    term = part[at * 16 : (at + 1) * 16]
-                    if (p == 4 or q == 4) and b == 0 and e == 0:
-                        acc[a, p, q] = term
-                    else:
-                        acc[a, p, q] += term
+                    acc[a, p, q] += part[at * 16 : (at + 1) * 16]
 
 
 def convolve(src, w, acc, half):
@@ -225,23 +222,40 @@
     kept[...] = jnp.dot(g_own[0:256], own, preferred_element_type=F32)
     load_halo.wait()
 
-    for copy in sent:
-        copy.wait_recv()
     has_up, has_down = row > 0, row < n_row - 1
     has_left, has_right = col > 0, col < n_col - 1
-    for start, count, there in (
-        (0, 4, has_up), (4, 4, has_down), (8, 4, has_left), (12, 4, has_right),
+
+    def norm_halo(parts):
+        for start, count, there in parts:
+            values = norm(halo[start : start + count].reshape(count * 16, CHANS))
+            values = values * jnp.where(there, 1.0, 0.0).astype(F32)
+            normed[start : start + count] = values.astype(BF16).reshape(count, 16, CHANS)
+
+    sides_at = 16 * len(SIDE_TILES)
+    for copy in sent[4:]:
+        copy.wait_recv()
+    norm_halo(((0, 4, has_up), (4, 4, has_down), (8, 4, has_left), (12, 4, has_right)))
+    spread = others[...] + jnp.dot(
+        g_halo[:, 0:256], normed[0:16].reshape(256, CHANS), preferred_element_type=F32
+    )
+    for at, (p, q) in enumerate(SIDE_TILES):
+        cells[p, q] = spread[at * 16 : (at + 1) * 16].astype(BF16)
+    others[sides_at:] = spread[sides_at:]
+    convolve_rest(cells, k1, acc, SIDE_TILES)
+
+    for copy in sent[:4]:
+        copy.wait_recv()
+    norm_halo((
         (16, 1, has_up & has_left), (17, 1, has_up & has_right),
         (18, 1, has_down & has_left), (19, 1, has_down & has_right),
-    ):
-        values = norm(halo[start : start + count].reshape(count * 16, CHANS))
-        values = values * jnp.where(there, 1.0, 0.0).astype(F32)
-        normed[start : start + count] = values.astype(BF16).reshape(count, 16, CHANS)
-    spread = others[...] + jnp.dot(g_halo[...], normed[...].reshape(384, CHANS), preferred_element_type=F32)
-    for at, (p, q) in enumerate(OTHER_TILES):
+    ))
+    spread = others[sides_at:] + jnp.dot(
+        g_halo[sides_at:, 256:384], normed[16:24].reshape(128, CHANS), preferred_element_type=F32
+    )
+    for at, (p, q) in enumerate(CORNER_TILES):
         cells[p, q] = spread[at * 16 : (at + 1) * 16].astype(BF16)
-
-    convolve_rest(cells, k1, acc)
+    convolve_rest(cells, k1, acc, CORNER_TILES)
+
     value = joined(acc, 5, 5)
     value = value / (1.0 + jnp.exp(-value))
     def flag(there):
@@ -357,8 +371,7 @@
                     for copy in near2[c, u]:
                         copy.wait_recv()
                 far2[c, u].wait_recv()
-            if move != ORDER[-1]:
-                multiply(c, which, range(3))
+            multiply(c, which, (0, 2))
 
     s = lax.broadcasted_iota(jnp.int32, (1, 16, OUT_DEV), 1) % 2
     edge = jnp.zeros((1, 16, OUT_DEV), F32)
@@ -375,7 +388,6 @@
     def pack(part):
         return jnp.concatenate([part[:8].reshape(64, OUT_DEV), part[8:].reshape(64, OUT_DEV)], axis=1)
 
-    multiply(c, which, (0, 2))
     above, below = moved(0), moved(2)
     u_out[0] = pack(below[:, 0])
     u_out[1] = pack(above[:, 1])
@@ -383,7 +395,8 @@
         send(u_out.at[0], u_in.at[1], u_send.at[0], u_recv.at[0], (up, col)),
         send(u_out.at[1], u_in.at[0], u_send.at[1], u_recv.at[1], (down, col)),
     ]
-    multiply(c, which, (1,))
+    for c in range(CHUNKS):
+        multiply(c, range(RING), (1,))
     load_mean.wait()
     centre = lat[col].reshape(256, CHANS)
     shortcut = jnp.dot(centre, g_mean[...], preferred_element_type=F32).reshape(PIECES, 2, 8, OUT_DEV)

time: 47 us -> 46.3 us (0.985)
  Pallas kernels: 45.3 us -> 44.7 us
    pallas_call x1, Pallas kernels: 45.3 us -> 44.7 us  [per_device(): pl.pallas_call(functools.partial(kernel, n_row, n_col), out_shape=jax.Sha...]
where the time goes in v5:
time: 46.3 us; the launch traced here: 46.2 us
  Pallas kernels  44.7 us (97%)
  local copies, waits for them, and re-layouts  1.52 us (3%)
    pallas_call x1, Pallas kernels, per_device(): pl.pallas_call(functools.partial(kernel, n_row, n_col), out_shape=jax.Sha...  44.7 us
    transpose x1, local copies, waits for them, and re-layouts, per_device(): return out.transpose(2, 0, 1, 3, 4).reshape(FRAMES, 2, 2 * PIECES, OUT_DEV)  1.52 us

profile of v5, /device:TPU:1, one launch (start us, length us, event | category | flops | bytes accessed | tf_op | source)
XLA Modules:
  0.0 46.2 jit_solution(437952769324173008)
XLA Ops:
  0.0 44.7 %shard_map.91 = bf16[2,128,64]{2,1,0:T(8,128)(2,1)} custom-call(bf16[4,4,16,256]{3,2,1,0:T(8,128)(2,1)} %bitcast.11, f32[1,256]{1,0:T(1,128)} %bitcast.12, bf16[3,3,3,256,256]{4,3,2,1,0:T(8,128)(2,1)} %k1_hbm.1, bf16[3,3,3,256,256]{4,3,2,1,0:T(8,128)(2,1)} %k2_hbm.1, bf16[3,192,4096]{2,1,0:T(8,128)(2,1)} %bitcast.10, ...), custom_call_target="tpu_custom_call" | custom-call | flops 4294967296 | bytes 14680064 | tf_op jit(solution)/shard_map/pallas_call | solution.py:426
  44.7 1.5 %copy.10 = bf16[4,2,16,2,64]{4,3,2,1,0:T(2,128)(2,1)} copy(bf16[4,2,16,2,64]{4,3,0,2,1:T(2,128)(2,1)} %bitcast.9) | data formatting | bytes 65536 | tf_op jit(solution)/shard_map/transpose | solution.py:484

commit v6 on v5

--- a/solution.py
+++ b/solution.py
@@ -19,7 +19,7 @@
 PARTS = ((0, 6, False), (6, 12, False), (12, 16, True))
 CHUNKS = len(PARTS)
 ORDER = (
-    ("C0", "C1", "n0", "n2", "d2", "N00", "n1", "N10", "e2", "f0", "N01", "N03", "f1", "N11", "N13", "N20", "N21", "N23", "N22")
+    ("C0", "n0", "N00", "C1", "n2", "d2", "n1", "N10", "e2", "f0", "N01", "N03", "f1", "N11", "N13", "N20", "N21", "N23", "N22")
     + ("F00", "F10", "D02", "D12", "F01", "F03", "F11", "F13", "F20", "F21", "F23", "F22", "W00132", "W10132", "W20132")
 )
 
@@ -159,8 +159,8 @@
 
     barrier = pltpu.get_barrier_semaphore()
     around = (
+        (up, left), (up, right), (down, left), (down, right),
         (up, col), (down, col), (row, left), (row, right),
-        (up, left), (up, right), (down, left), (down, right),
     ) + to_z + to_y + (to_z2, to_y2)
     for target in around:
         pl.semaphore_signal(barrier, inc=1, device_id=target, device_id_type=MESH)

time: 46.3 us -> 46.1 us (level)
  no operation moved by 1% of the time
where the time goes in v6:
time: 46.1 us; the launch traced here: 46 us
  Pallas kernels  44.4 us (96%)
  local copies, waits for them, and re-layouts  1.52 us (3%)
    pallas_call x1, Pallas kernels, per_device(): pl.pallas_call(functools.partial(kernel, n_row, n_col), out_shape=jax.Sha...  44.4 us
    transpose x1, local copies, waits for them, and re-layouts, per_device(): return out.transpose(2, 0, 1, 3, 4).reshape(FRAMES, 2, 2 * PIECES, OUT_DEV)  1.52 us

profile of v6, /device:TPU:1, one launch (start us, length us, event | category | flops | bytes accessed | tf_op | source)
XLA Modules:
  0.0 46.0 jit_solution(5356523559104856871)
XLA Ops:
  0.0 44.4 %shard_map.91 = bf16[2,128,64]{2,1,0:T(8,128)(2,1)} custom-call(bf16[4,4,16,256]{3,2,1,0:T(8,128)(2,1)} %bitcast.11, f32[1,256]{1,0:T(1,128)} %bitcast.12, bf16[3,3,3,256,256]{4,3,2,1,0:T(8,128)(2,1)} %k1_hbm.1, bf16[3,3,3,256,256]{4,3,2,1,0:T(8,128)(2,1)} %k2_hbm.1, bf16[3,192,4096]{2,1,0:T(8,128)(2,1)} %bitcast.10, ...), custom_call_target="tpu_custom_call" | custom-call | flops 4294967296 | bytes 14680064 | tf_op jit(solution)/shard_map/pallas_call | solution.py:426
  44.5 1.5 %copy.10 = bf16[4,2,16,2,64]{4,3,2,1,0:T(2,128)(2,1)} copy(bf16[4,2,16,2,64]{4,3,0,2,1:T(2,128)(2,1)} %bitcast.9) | data formatting | bytes 65536 | tf_op jit(solution)/shard_map/transpose | solution.py:484

commit v7 on v6

--- a/solution.py
+++ b/solution.py
@@ -19,7 +19,7 @@
 PARTS = ((0, 6, False), (6, 12, False), (12, 16, True))
 CHUNKS = len(PARTS)
 ORDER = (
-    ("C0", "n0", "N00", "C1", "n2", "d2", "n1", "N10", "e2", "f0", "N01", "N03", "f1", "N11", "N13", "N20", "N21", "N23", "N22")
+    ("C0", "n0", "N00", "C1", "n2", "d2", "n1", "N10", "f0", "N01", "N03", "f1", "N11", "N13", "e2", "N20", "N21", "N23", "N22")
     + ("F00", "F10", "D02", "D12", "F01", "F03", "F11", "F13", "F20", "F21", "F23", "F22", "W00132", "W10132", "W20132")
 )
 

time: 46.1 us -> 46.1 us (level)
  no operation moved by 1% of the time
where the time goes in v7:
time: 46.1 us; the launch traced here: 46 us
  Pallas kernels  44.5 us (97%)
  local copies, waits for them, and re-layouts  1.52 us (3%)
    pallas_call x1, Pallas kernels, per_device(): pl.pallas_call(functools.partial(kernel, n_row, n_col), out_shape=jax.Sha...  44.5 us
    transpose x1, local copies, waits for them, and re-layouts, per_device(): return out.transpose(2, 0, 1, 3, 4).reshape(FRAMES, 2, 2 * PIECES, OUT_DEV)  1.52 us

profile of v7, /device:TPU:1, one launch (start us, length us, event | category | flops | bytes accessed | tf_op | source)
XLA Modules:
  0.0 46.0 jit_solution(13641073967941923813)
XLA Ops:
  0.0 44.5 %shard_map.91 = bf16[2,128,64]{2,1,0:T(8,128)(2,1)} custom-call(bf16[4,4,16,256]{3,2,1,0:T(8,128)(2,1)} %bitcast.11, f32[1,256]{1,0:T(1,128)} %bitcast.12, bf16[3,3,3,256,256]{4,3,2,1,0:T(8,128)(2,1)} %k1_hbm.1, bf16[3,3,3,256,256]{4,3,2,1,0:T(8,128)(2,1)} %k2_hbm.1, bf16[3,192,4096]{2,1,0:T(8,128)(2,1)} %bitcast.10, ...), custom_call_target="tpu_custom_call" | custom-call | flops 4294967296 | bytes 14680064 | tf_op jit(solution)/shard_map/pallas_call | solution.py:426
  44.5 1.5 %copy.10 = bf16[4,2,16,2,64]{4,3,2,1,0:T(2,128)(2,1)} copy(bf16[4,2,16,2,64]{4,3,0,2,1:T(2,128)(2,1)} %bitcast.9) | data formatting | bytes 65536 | tf_op jit(solution)/shard_map/transpose | solution.py:484

commit v8 on v7

--- a/solution.py
+++ b/solution.py
@@ -19,7 +19,7 @@
 PARTS = ((0, 6, False), (6, 12, False), (12, 16, True))
 CHUNKS = len(PARTS)
 ORDER = (
-    ("C0", "n0", "N00", "C1", "n2", "d2", "n1", "N10", "f0", "N01", "N03", "f1", "N11", "N13", "e2", "N20", "N21", "N23", "N22")
+    ("C0", "n0", "N00", "C1", "n1", "n2", "d2", "N10", "e2", "f0", "N01", "N03", "f1", "N11", "N13", "N20", "N21", "N23", "N22")
     + ("F00", "F10", "D02", "D12", "F01", "F03", "F11", "F13", "F20", "F21", "F23", "F22", "W00132", "W10132", "W20132")
 )
 

time: 46.1 us -> 46.1 us (level)
  no operation moved by 1% of the time
where the time goes in v8:
time: 46.1 us; the launch traced here: 46 us
  Pallas kernels  44.4 us (96%)
  local copies, waits for them, and re-layouts  1.52 us (3%)
    pallas_call x1, Pallas kernels, per_device(): pl.pallas_call(functools.partial(kernel, n_row, n_col), out_shape=jax.Sha...  44.4 us
    transpose x1, local copies, waits for them, and re-layouts, per_device(): return out.transpose(2, 0, 1, 3, 4).reshape(FRAMES, 2, 2 * PIECES, OUT_DEV)  1.52 us

profile of v8, /device:TPU:1, one launch (start us, length us, event | category | flops | bytes accessed | tf_op | source)
XLA Modules:
  0.0 46.0 jit_solution(9857479977257238660)
XLA Ops:
  0.0 44.4 %shard_map.91 = bf16[2,128,64]{2,1,0:T(8,128)(2,1)} custom-call(bf16[4,4,16,256]{3,2,1,0:T(8,128)(2,1)} %bitcast.11, f32[1,256]{1,0:T(1,128)} %bitcast.12, bf16[3,3,3,256,256]{4,3,2,1,0:T(8,128)(2,1)} %k1_hbm.1, bf16[3,3,3,256,256]{4,3,2,1,0:T(8,128)(2,1)} %k2_hbm.1, bf16[3,192,4096]{2,1,0:T(8,128)(2,1)} %bitcast.10, ...), custom_call_target="tpu_custom_call" | custom-call | flops 4294967296 | bytes 14680064 | tf_op jit(solution)/shard_map/pallas_call | solution.py:426
  44.5 1.5 %copy.10 = bf16[4,2,16,2,64]{4,3,2,1,0:T(2,128)(2,1)} copy(bf16[4,2,16,2,64]{4,3,0,2,1:T(2,128)(2,1)} %bitcast.9) | data formatting | bytes 65536 | tf_op jit(solution)/shard_map/transpose | solution.py:484
